TPU v7x, 32 devices: a whole 2x2x4 slice. The times are simulated.
32 devices in a mesh: grp: 2 (over x), feat: 16 (over z, y, core).
Axes of the slice: x: 2, y: 2, z: 4, core: 2. Of those that a mesh axis runs over, the one named last changes fastest.
Arguments:
- x_acts: bfloat16 [8, 1024, 4096], P('grp'), parts along dimension 0, may hold values from -6 to 6
- delta: bfloat16 [8, 1024, 4096], P('grp', None, 'feat'), parts along dimension 0, may hold values from -6 to 6
- pattern: int32 [32, 32], replicated, may hold values 0 or 1
- row_signs: int32 [4096], replicated, may hold values from -1 to 1, as said below
- col_signs: int32 [4096], replicated, may hold values from -1 to 1, as said below
- cols: int32 [8192], replicated, may hold values from 0 to 16777215
Outputs:
- sketch: float32 [8, 8192], P('grp'), parts along dimension 0
There are 2 independent parts, one for each index of `grp`. A program takes and returns all parts, laid end to end along the dimension named above; an argument that names none is the same for every part. Nothing has to cross between parts.
Inputs may be any that keep to these rules, and one draw needn't show every extreme that they name: `row_signs`: every entry is -1 or +1. `col_signs`: every entry is -1 or +1.
All inputs are finite; a program needn't handle non-finite values.
Results may differ from a plain program's by a relative error of at most 0.0029.
Values may be sent and summed in bfloat16 or wider, within the bound.
A program may use at most 192 MiB of HBM per device.

v0:
```python
import math

import jax
import jax.numpy as jnp
from jax import lax
from jax.sharding import PartitionSpec as P

BLK = 128
SKETCH = 8192


def partner(value, axis, apart):
    mask = 2**apart
    pairs = [(source, source ^ mask) for source in range(lax.axis_size(axis))]
    return lax.ppermute(value, axis, pairs)


def hadamard(mat_order):
    row_ids = lax.iota(jnp.int32, mat_order)[:, None]
    col_ids = lax.iota(jnp.int32, mat_order)[None, :]
    intersection = row_ids & col_ids
    parity = jnp.zeros((mat_order, mat_order), jnp.int32)
    for bit_pos in range(max(mat_order - 1, 0).bit_length()):
        parity = parity ^ intersection >> bit_pos & 1
    return (1 - 2 * parity).astype(jnp.float32)


def parity_sign(left_ids, right_ids, n_bits):
    intersection = left_ids & right_ids
    parity = jnp.zeros_like(intersection)
    for bit_pos in range(n_bits):
        parity = parity ^ intersection >> bit_pos & 1
    return (1 - 2 * parity).astype(jnp.float32)


def build_mask(global_rows, pattern, width_in):
    row_select = (
        (global_rows // BLK)[:, None] == lax.iota(jnp.int32, pattern.shape[0])[None, :]
    ).astype(jnp.float32)
    col_block = lax.iota(jnp.int32, width_in) // BLK
    col_select = (lax.iota(jnp.int32, pattern.shape[1])[:, None] == col_block[None, :]).astype(
        jnp.float32
    )
    return jnp.dot(jnp.dot(row_select, pattern.astype(jnp.float32)), col_select)


def signed_gradient(delta_part, acts_part, global_rows, sign_rows, pattern, col_signs):
    tokens_each = acts_part.shape[1]
    width_in = acts_part.shape[2]
    block_mask = build_mask(global_rows, pattern, width_in)
    gradient = (
        jnp.einsum("etr,etc->erc", delta_part, acts_part, preferred_element_type=jnp.float32)
        / tokens_each
    )
    gradient = (gradient * block_mask[None]).astype(jnp.bfloat16)
    sign_table = (sign_rows[:, None] * col_signs[None, :]).astype(jnp.bfloat16)
    return gradient * sign_table[None]


def column_section(signed):
    examples, rows_here, width_in = signed.shape
    low_width = min(128, width_in)
    high_width = width_in // low_width
    shaped = signed.reshape(examples, rows_here, high_width, low_width)
    section = jnp.einsum(
        "erqj,jk->erqk",
        shaped,
        hadamard(low_width).astype(jnp.bfloat16),
        preferred_element_type=jnp.float32,
    )
    section = jnp.einsum(
        "erqk,qp->pker", section, hadamard(high_width), precision=lax.Precision.HIGHEST
    )
    return section.reshape(width_in, examples, rows_here)


def kept_entries(section, global_rows, cols, width_in, width_out):
    row_bits = max(width_out - 1, 0).bit_length()
    weight = parity_sign(global_rows[:, None], (cols // width_in)[None, :], row_bits)
    picked = jnp.take(section, cols % width_in, axis=0)
    return jnp.einsum("ker,rk->ek", picked, weight, precision=lax.Precision.HIGHEST)


def per_device(x_acts, delta, pattern, row_signs, col_signs, cols):
    examples, tokens_each, width_in = x_acts.shape
    local_rows = delta.shape[2]
    feat_count = lax.axis_size("feat")
    my_index = lax.axis_index("feat")
    width_out = local_rows * feat_count
    group_size = max(feat_count // examples, 1)
    held = max(examples // feat_count, 1)
    sub_rows = local_rows // group_size
    pieces = delta.reshape(examples, tokens_each, group_size, sub_rows)
    pieces = pieces.transpose(0, 2, 1, 3).reshape(examples * group_size, tokens_each, sub_rows)
    regrouped = lax.all_to_all(pieces, "feat", split_axis=0, concat_axis=2, tiled=True)
    slot = my_index % group_size
    first_example = my_index // group_size * held
    acts_mine = lax.dynamic_slice_in_dim(x_acts, first_example, held, 0)
    position = lax.iota(jnp.int32, feat_count * sub_rows)
    global_rows = position // sub_rows * local_rows + slot * sub_rows + position % sub_rows
    sign_rows = jnp.take(row_signs, global_rows)
    signed = signed_gradient(regrouped, acts_mine, global_rows, sign_rows, pattern, col_signs)
    section = column_section(signed)
    partial_value = kept_entries(section, global_rows, cols, width_in, width_out)
    for bit_pos in range(max(group_size - 1, 0).bit_length()):
        partial_value = partial_value + partner(partial_value, "feat", bit_pos)
    part_len = SKETCH // group_size
    mine = lax.dynamic_slice_in_dim(partial_value, slot * part_len, part_len, 1)
    gathered = lax.all_gather(mine[None], "feat", axis=0, tiled=True)
    total = gathered.reshape(feat_count // group_size, group_size, held, part_len)
    total = total.transpose(0, 2, 1, 3).reshape(examples, SKETCH)
    return total / math.sqrt(SKETCH)


def solution(mesh):
    placed = (P("grp", None, None), P("grp", None, "feat"), P(), P(), P(), P())
    return jax.shard_map(
        per_device, mesh=mesh, in_specs=placed, out_specs=P("grp", None), check_vma=False
    )
```

profile of v0, /device:TPU:0, one launch (start us, length us, event | category | flops | bytes accessed | tf_op | source)
XLA Modules:
  0.0 283.9 jit_solution(2217800679359277054)
XLA Ops:
  0.0 2.9 %fusion.111 = (bf16[4,1024,64]{2,1,0:T(8,128)(2,1)S(1)}, bf16[4,1024,64]{2,1,0:T(8,128)(2,1)S(1)}, bf16[4,1024,64]{2,1,0:T(8,128)(2,1)S(1)}, bf16[4,1024,64]{2,1,0:T(8,128)(2,1)S(1)}) fusion(bf16[4,1024,256]{2,1,0:T(8,128)(2,1)} %param.7), kind=kLoop, calls=%fused_computation.160 | loop fusion | bytes 4194304 | tf_op jit(solution)/shard_map/slice
  3.0 2.4 pad_maximum_fusion
  5.3 4.8 %copy.13 = bf16[16,1024,64]{1,2,0:T(8,128)(2,1)} copy(bf16[16,1024,64]{2,1,0:T(8,128)(2,1)} %bitcast.36) | data formatting | bytes 4194304 | tf_op jit(solution)/shard_map/reshape | solution.py:94
  10.1 7.4 %all-to-all-start = ((bf16[16,1024,64]{1,2,0:T(8,128)(2,1)}), bf16[16,1024,64]{1,2,0:T(8,128)(2,1)S(1)}, u32[]{:S(2)}, u32[]{:S(2)}) async-start(bf16[16,1024,64]{1,2,0:T(8,128)(2,1)} %copy.13), calls=%async_computation | async-start | bytes 4194304 | tf_op jit(solution)/shard_map/all_to_all | solution.py:95
  17.5 0.8 broadcast_clamp_fusion
  18.3 43.8 %fusion.15 = f32[8192,1024]{0,1:T(8,128)} fusion(s32[8192]{0:T(1024)S(1)} %get-tuple-element.10, s32[1024]{0:T(1024)S(1)} %fusion.92), kind=kLoop, calls=%fused_computation.29 | loop fusion | flops 327155712 | bytes 33591296
  62.2 33.5 %copy.19 = f32[8192,1024]{1,0:T(8,128)} copy(f32[8192,1024]{0,1:T(8,128)} %fusion.15) | data formatting | bytes 67108864
  95.7 6.2 %gather_fusion = s32[1024]{0:T(1024)S(1)} fusion(s32[4096]{0:T(1024)S(1)} %copy-done, s32[1024]{0:T(1024)S(1)} %broadcast_clamp_fusion.1), kind=kCustom, calls=%fused_computation | custom fusion | bytes 12288 | tf_op jit(solution)/shard_map/jit(_take)/gather | solution.py:101
  101.9 7.3 %fusion.33 = f32[1024,4096]{1,0:T(8,128)} fusion(s32[4096]{0:T(1024)S(1)} %add_select_fusion.2, s32[1024]{0:T(1024)S(1)} %get-tuple-element.11, s32[32,32]{1,0:T(8,128)S(1)} %copy-done.3), kind=kOutput, calls=%fused_computation.50 | convolution fusion | flops 270697472 | bytes 16801792 | tf_op jit(solution)/shard_map/dot_general | solution.py:44
  109.3 0.0 all-to-all-done
  109.3 16.8 %fusion.28 = bf16[128,8,32,128]{3,1,2,0:T(8,128)(2,1)} fusion(s32[4096]{0:T(1024)S(1)} %copy-done.4, s32[1024]{0:T(1024)S(1)} %get-tuple-element.12, f32[1024,4096]{1,0:T(8,128)} %fusion.33, bf16[1024,1024]{0,1:T(8,128)(2,1)S(1)} %bitcast.37, bf16[4,1024,4096]{2,1,0:T(8,128)(2,1)} %param.6, s32[]{:T(128)S(6)} %select_n.139), kind=kOutput, calls=%fused_computation.46 | convolution fusion | flops 8615100416 | bytes 35672068 | tf_op jit(solution)/shard_map/etr,etc->erc/dot_general | solution.py:52
  126.1 9.4 %copy.23 = bf16[128,8,32,128]{3,2,1,0:T(8,128)(2,1)} copy(bf16[128,8,32,128]{3,1,2,0:T(8,128)(2,1)} %fusion.28) | data formatting | bytes 16777216
  135.5 11.5 %fusion.40 = f32[1024,32,128]{2,1,0:T(8,128)} fusion(bf16[1024,32,128]{2,1,0:T(8,128)(2,1)} %bitcast.35), kind=kOutput, calls=%fused_computation.65 | convolution fusion | flops 1074151424 | bytes 25165824 | tf_op jit(solution)/shard_map/erqj,jk->erqk/dot_general | solution.py:65
  147.0 21.4 %convolution_bitcast_fusion = f32[32,128,1,1024]{1,0,3,2:T(8,128)} fusion(f32[1024,32,128]{2,1,0:T(8,128)} %fusion.40), kind=kOutput, calls=%fused_computation.44 | convolution fusion | flops 1610631168 | bytes 33554432 | tf_op jit(solution)/shard_map/erqk,qp->pker/dot_general | solution.py:71
  168.4 16.5 %copy.22 = f32[32,128,1,1024]{3,1,0,2:T(8,128)} copy(f32[32,128,1,1024]{1,0,3,2:T(8,128)} %convolution_bitcast_fusion) | data formatting | bytes 33554432 | tf_op jit(solution)/shard_map/reshape | solution.py:74
  184.9 49.4 %gather_fusion.1 = f32[8192,1024]{1,0:T(8,128)} fusion(f32[4096,1024]{1,0:T(8,128)} %bitcast.34, s32[8192]{0:T(1024)S(1)} %get-tuple-element.9), kind=kCustom, calls=%fused_computation.1 | custom fusion | bytes 67141632 | tf_op jit(solution)/shard_map/jit(_take)/gather | solution.py:80
  234.3 21.1 %multiply_reduce_fusion = f32[8192]{0:T(1024)S(1)} fusion(f32[8192,1024]{1,0:T(8,128)} %copy.19, f32[8192,1024]{1,0:T(8,128)} %gather_fusion.1, pred[8192]{0:T(1024)(128)(4,1)S(1)} %compare_and_fusion), kind=kLoop, calls=%fused_computation.41 | loop fusion | flops 25157632 | bytes 67149824 | tf_op jit(solution)/shard_map/ker,rk->ek/dot_general | solution.py:81
  255.4 0.5 collective-permute-start
  255.9 0.9 collective-permute-done
  256.8 1.9 collective-permute-start.1
  258.7 2.1 collective-permute-done.1
  260.7 22.0 %all-gather.1 = f32[16,1,2048]{2,1,0:T(1,128)S(1)} all-gather(f32[1,1,2048]{2,1,0:T(1,128)S(1)} %fusion.77), channel_id=2, replica_groups=mesh['grp'=2,'feat'=16] {'feat'}, dimensions={0}, use_global_device_ids=true | all-gather | bytes 139264 | tf_op jit(solution)/shard_map/all_gather | solution.py:109
  282.8 0.4 multiply_reduce_fusion.1
  283.1 0.7 div.85
  (18 shorter events, 0.1 us)
Async XLA Ops:
  0.0 95.7 %copy-start = (s32[4096]{0:T(1024)S(1)}, s32[4096]{0:T(1024)}, u32[]{:S(2)}) copy-start(s32[4096]{0:T(1024)} %param.9) | copy-start | bytes 49156
  10.1 99.2 %all-to-all-start = ((bf16[16,1024,64]{1,2,0:T(8,128)(2,1)}), bf16[16,1024,64]{1,2,0:T(8,128)(2,1)S(1)}, u32[]{:S(2)}, u32[]{:S(2)}) async-start(bf16[16,1024,64]{1,2,0:T(8,128)(2,1)} %copy.13), calls=%async_computation | async-start | bytes 4194304 | tf_op jit(solution)/shard_map/all_to_all | solution.py:95
  62.2 39.7 %copy-start.2 = (s32[8192]{0:T(1024)S(1)}, s32[8192]{0:T(1024)}, u32[]{:S(2)}) copy-start(s32[8192]{0:T(1024)} %param.11) | copy-start | bytes 98308
  62.2 39.8 %copy-start.3 = (s32[32,32]{1,0:T(8,128)S(1)}, s32[32,32]{1,0:T(8,128)}, u32[]{:S(2)}) copy-start(s32[32,32]{1,0:T(8,128)} %param.8) | copy-start | bytes 12292
  62.2 47.1 %copy-start.4 = (s32[4096]{0:T(1024)S(1)}, s32[4096]{0:T(1024)}, u32[]{:S(2)}) copy-start(s32[4096]{0:T(1024)} %param.10) | copy-start | bytes 49156
  184.9 98.9 %copy-start.1 = (s32[4096]{0:T(1024)S(1)}, s32[4096]{0:T(1024)}, u32[]{:S(2)}) copy-start(s32[4096]{0:T(1024)} %param.9) | copy-start | bytes 49156
  255.4 1.3 collective-permute-start
  256.8 4.0 %collective-permute-start.1 = (f32[1,8192]{1,0:T(1,128)S(1)}, f32[1,8192]{1,0:T(1,128)S(1)}, u32[]{:S(2)}, u32[]{:S(2)}) collective-permute-start(f32[1,8192]{1,0:T(1,128)S(1)} %add.176), channel_id=1, source_target_pairs={{0,2},{1,3},{2,0},{3,1},{4,6},{5,7},{6,4},{7,5},{8,10},{9,11},{10,... | collective-permute-start | bytes 98312 | tf_op jit(solution)/shard_map/ppermute | solution.py:15
where the time goes:
time: 285 us; the launch traced here: 284 us
  local copies, waits for them, and re-layouts  123 us (43%)
  other arithmetic  68.6 us (24%)
  matrix products  57 us (20%)
  blocking collectives  22 us (8%)
  starting transfers between devices  9.77 us (3%)
  waiting for transfers between devices  2.92 us (1%)
    gather x1, local copies, waits for them, and re-layouts, kept_entries(): picked = jnp.take(section, cols % width_in, axis=0)  49.4 us
    unnamed x2, other arithmetic  43.8 us
    unnamed x12, local copies, waits for them, and re-layouts  42.9 us
    all_gather x1, blocking collectives, per_device(): gathered = lax.all_gather(mine[None], 'feat', axis=0, tiled=True)  22 us
    dot_general x1, matrix products, column_section(): jnp.einsum('erqk,qp->pker', section, hadamard(high_width), precision=lax....  21.4 us
    dot_general x1, other arithmetic, kept_entries(): jnp.einsum('ker,rk->ek', picked, weight, precision=lax.Precision.HIGHEST)  21.1 us
    dot_general x1, matrix products, signed_gradient(): jnp.einsum('etr,etc->erc', delta_part, acts_part, preferred_element_type=...  16.8 us
    reshape x1, local copies, waits for them, and re-layouts, column_section(): return section.reshape(width_in, examples, rows_here)  16.5 us
  transfers between devices with their start and end apart: 3, of which 2 were waited for; matrix products, arithmetic and copies ran while one was open for 32% of the time, Pallas kernels for 0%

commit v1 on v0

v1 whole, which is shorter than its diff:
```python
import functools
import math

import jax
import jax.numpy as jnp
from jax import lax
from jax.experimental import pallas as pl
from jax.experimental.pallas import tpu as pltpu
from jax.sharding import PartitionSpec as P

BLK = 128
LANES = 128
TILE = 256
CHUNK = 512
F32 = jnp.float32
BF16 = jnp.bfloat16
NT = (((1,), (1,)), ((), ()))


def parity(value, bits):
    shift = 1
    while shift < bits:
        shift *= 2
    while shift > 1:
        shift //= 2
        value = value ^ (value >> shift)
    return value & 1


def sign_of(left, right, bits):
    return (1 - 2 * parity(left & right, bits)).astype(F32)


def iota(shape, axis):
    return lax.broadcasted_iota(jnp.int32, shape, axis)


def plan(cols_ref, tp_ref, lp_ref, rc_ref, info_v, info_s, rank_ref, sem, bins, width, rows, tiles):
    n_rows = cols_ref.shape[0]
    before = (iota((TILE, TILE), 0) < iota((TILE, TILE), 1)).astype(F32).astype(BF16)
    every = jnp.ones((TILE, TILE), BF16)
    bin_ids = iota((bins, TILE), 0)

    def hits(a):
        block = (cols_ref[pl.ds(a, 1), :] % width) // LANES
        return (bin_ids == block).astype(F32)

    def count(a, running):
        hit = hits(a)
        hit16 = hit.astype(BF16)
        ahead = jnp.dot(hit16, before, preferred_element_type=F32)
        total = jnp.dot(hit16, every, preferred_element_type=F32)
        rank = jnp.sum(hit * (ahead + running), axis=0, keepdims=True)
        rank_ref[pl.ds(a, 1), :] = rank.astype(jnp.int32)
        return running + total

    counts = lax.fori_loop(0, n_rows, count, jnp.zeros((bins, TILE), F32), unroll=8)
    need = (counts.astype(jnp.int32) + (TILE - 1)) // TILE
    lower = (iota((bins, bins), 1) < iota((bins, bins), 0)).astype(F32).astype(BF16)
    start = jnp.dot(lower, need.astype(F32).astype(BF16), preferred_element_type=F32)
    ends = start.astype(jnp.int32) + need
    tile_ids = iota((bins, LANES), 1)
    owner = jnp.sum((ends[:, :LANES] <= tile_ids).astype(jnp.int32), axis=0, keepdims=True)
    owner = jnp.minimum(owner, bins - 1)
    used = ends[bins - 1 :, :LANES]
    info_v[...] = jnp.where(iota((8, LANES), 0) == 0, owner, used)
    copy = pltpu.make_async_copy(info_v, info_s, sem)
    copy.start()

    slots = 2 * tiles
    slot_ids = iota((slots, TILE), 0)
    lane_ids = iota((LANES, TILE), 0)

    def place(a, acc):
        first = jnp.sum(hits(a) * start, axis=0, keepdims=True).astype(jnp.int32)
        rank = rank_ref[pl.ds(a, 1), :]
        lane = rank % TILE
        slot = first + rank // TILE + (lane // LANES) * tiles
        lane = lane % LANES
        tp_ref[pl.ds(a, 1), :] = slot
        lp_ref[pl.ds(a, 1), :] = lane
        cols = cols_ref[pl.ds(a, 1), :]
        row = ((cols // width) % rows).astype(F32)
        col = (cols % LANES).astype(F32)
        here = slot_ids == slot
        left = jnp.concatenate([jnp.where(here, row, 0.0), jnp.where(here, col, 0.0)], axis=0)
        right = (lane_ids == lane).astype(F32)
        return acc + lax.dot_general(
            left.astype(BF16), right.astype(BF16), NT, preferred_element_type=F32
        )

    acc = lax.fori_loop(0, n_rows, place, jnp.zeros((2 * slots, LANES), F32), unroll=4)
    acc = acc.astype(jnp.int32)
    for v in range(2):
        part = acc[v * slots : (v + 1) * slots]
        rc_ref[v] = jnp.concatenate([part[:tiles], part[tiles:]], axis=1)
    copy.wait()


def butterfly(g_ref, bins):
    def slab(s, carry):
        rows = pl.ds(pl.multiple_of(s * 8, 8), 8)
        parts = [g_ref[rows, c * LANES : (c + 1) * LANES] for c in range(bins)]
        half = 1
        while half < bins:
            for c in range(bins):
                if not c & half:
                    low, high = parts[c], parts[c + half]
                    parts[c], parts[c + half] = low + high, low - high
            half *= 2
        for c in range(bins):
            g_ref[rows, c * LANES : (c + 1) * LANES] = parts[c]
        return carry

    lax.fori_loop(0, g_ref.shape[0] // 8, slab, 0)


def tile_values(t, rc_ref, info_s, t1_ref, so_ref):
    examples, _, rows = t1_ref.shape[1:]
    row = rc_ref[0, pl.ds(t, 1), :]
    col = rc_ref[1, pl.ds(t, 1), :]
    low_ids = iota((16, TILE), 0)
    row_low = sign_of(low_ids, row % 16, 4).astype(BF16)
    high_bits = rows // 16
    row_high = sign_of(iota((max(high_bits, 8), TILE), 0), row // 16, 8).astype(BF16)
    weight = jnp.concatenate([row_low * row_high[h : h + 1] for h in range(high_bits)], axis=0)
    block = t1_ref[info_s[0, t]].reshape(examples * LANES, rows)
    value = jnp.dot(block, weight, preferred_element_type=F32)
    col_low = sign_of(iota((8, TILE), 0), col % 8, 3)
    col_high = sign_of(iota((16, TILE), 0), col // 8, 4)
    for e in range(examples):
        total = jnp.zeros((8, TILE), F32)
        for h in range(16):
            at = e * LANES + h * 8
            total = total + value[at : at + 8] * col_high[h : h + 1]
        so_ref[e, pl.ds(t, 1), :] = jnp.sum(total * col_low, axis=0, keepdims=True)


def unplace(me, cols_ref, tp_ref, lp_ref, so_ref, out_ref, width, rows, tiles):
    examples = so_ref.shape[0]
    flipped = []
    for e in range(examples):
        one = so_ref[e]
        both = jnp.concatenate([one[:, :LANES], one[:, LANES:]], axis=0)
        flipped.append(both.T)
    table = jnp.concatenate(flipped, axis=0).astype(BF16)
    slot_ids = iota((2 * tiles, CHUNK), 0)
    lane_ids = iota((LANES, CHUNK), 0)

    def wide(ref, a):
        return jnp.concatenate([ref[pl.ds(2 * a, 1), :], ref[pl.ds(2 * a + 1, 1), :]], axis=1)

    def chunk(a, carry):
        pick = (slot_ids == wide(tp_ref, a)).astype(F32).astype(BF16)
        spread = jnp.dot(table, pick, preferred_element_type=F32)
        mine = lane_ids == wide(lp_ref, a)
        high = wide(cols_ref, a) // (width * rows)
        sign = sign_of(high, me, 16)
        kept = [
            jnp.sum(jnp.where(mine, spread[e * LANES : (e + 1) * LANES], 0.0), axis=0, keepdims=True) * sign
            for e in range(examples)
        ]
        lines = [
            kept[e][:, q * LANES : (q + 1) * LANES]
            for q in range(CHUNK // LANES)
            for e in range(examples)
        ]
        out_ref[a] = jnp.concatenate(lines, axis=0).astype(BF16)
        return carry

    lax.fori_loop(0, out_ref.shape[0], chunk, 0, unroll=2)


def sketch_kernel(
    bins, tiles, me_ref, x_ref, delta_ref, rs_ref, cf_ref, cols_ref, out_ref,
    dt_ref, g_ref, t1_ref, tp_ref, lp_ref, rank_ref, rc_ref, so_ref, info_v, info_s, sem,
):
    e, nb = pl.program_id(0), pl.program_id(1)
    rows, width = g_ref.shape
    step_cols = x_ref.shape[2]

    @pl.when((e == 0) & (nb == 0))
    def _():
        plan(cols_ref, tp_ref, lp_ref, rc_ref, info_v, info_s, rank_ref, sem, bins, width, rows, tiles)

    @pl.when(nb == 0)
    def _():
        dt_ref[...] = (delta_ref[0] * rs_ref[...]).T

    acc = jnp.dot(dt_ref[...], x_ref[0], preferred_element_type=F32)
    at = pl.ds(pl.multiple_of(nb * step_cols, step_cols), step_cols)
    per = min(rows, BLK)
    for b in range(rows // per):
        part = acc[b * per : (b + 1) * per] * cf_ref[b : b + 1, :]
        g_ref[b * per : (b + 1) * per, at] = part.astype(BF16).astype(F32)

    @pl.when(nb == pl.num_programs(1) - 1)
    def _():
        butterfly(g_ref, bins)
        for c in range(bins):
            t1_ref[c, e] = g_ref[:, c * LANES : (c + 1) * LANES].astype(BF16).T

    @pl.when((e == pl.num_programs(0) - 1) & (nb == pl.num_programs(1) - 1))
    def _():
        so_ref[...] = jnp.zeros_like(so_ref)

        def four(s, carry):
            for u in range(4):
                tile_values(s * 4 + u, rc_ref, info_s, t1_ref, so_ref)
            return carry

        lax.fori_loop(0, (info_s[1, 0] + 3) // 4, four, 0)
        unplace(me_ref[0], cols_ref, tp_ref, lp_ref, so_ref, out_ref, width, rows, tiles)


def local_sketch(me, x_acts, delta, row_sign, col_factor, cols):
    examples, tokens, width = x_acts.shape
    rows = delta.shape[2]
    sketch = cols.shape[0]
    bins = width // LANES
    tiles = sketch // TILE + bins
    step_cols = 1024
    smem = pl.BlockSpec(memory_space=pltpu.SMEM)
    whole = lambda shape: pl.BlockSpec(shape, lambda e, n: (0,) * len(shape))
    lines = CHUNK // LANES * examples
    out_shape = (sketch // CHUNK, lines, LANES)
    return pl.pallas_call(
        functools.partial(sketch_kernel, bins, tiles),
        grid=(examples, width // step_cols),
        out_shape=jax.ShapeDtypeStruct(out_shape, BF16),
        in_specs=[
            smem,
            pl.BlockSpec((1, tokens, step_cols), lambda e, n: (e, 0, n)),
            pl.BlockSpec((1, tokens, rows), lambda e, n: (e, 0, 0)),
            whole((1, rows)),
            pl.BlockSpec((col_factor.shape[0], step_cols), lambda e, n: (0, n)),
            whole((sketch // TILE, TILE)),
        ],
        out_specs=whole(out_shape),
        scratch_shapes=[
            pltpu.VMEM((rows, tokens), BF16),
            pltpu.VMEM((rows, width), F32),
            pltpu.VMEM((bins, examples, LANES, rows), BF16),
            pltpu.VMEM((sketch // TILE, TILE), jnp.int32),
            pltpu.VMEM((sketch // TILE, TILE), jnp.int32),
            pltpu.VMEM((sketch // TILE, TILE), jnp.int32),
            pltpu.VMEM((2, tiles, TILE), jnp.int32),
            pltpu.VMEM((examples, tiles, TILE), F32),
            pltpu.VMEM((8, LANES), jnp.int32),
            pltpu.SMEM((8, LANES), jnp.int32),
            pltpu.SemaphoreType.DMA,
        ],
        compiler_params=pltpu.CompilerParams(vmem_limit_bytes=48 * 2**20),
        cost_estimate=pl.CostEstimate(
            flops=2 * examples * tokens * width * rows,
            bytes_accessed=2 * examples * tokens * (width + rows),
            transcendentals=0,
        ),
    )(me, x_acts, delta, row_sign, col_factor, cols.reshape(sketch // TILE, TILE))


def sum_kernel(n, part_ref, out_ref, recv, send1, recv1, send2, recv2):
    me = lax.axis_index("feat")
    barrier = pltpu.get_barrier_semaphore()

    def other(o):
        return lax.rem(me + o, n)

    def greet(o, carry):
        pl.semaphore_signal(
            barrier, inc=1, device_id={"feat": other(o)}, device_id_type=pl.DeviceIdType.MESH
        )
        return carry

    lax.fori_loop(1, n, greet, 0)
    pl.semaphore_wait(barrier, n - 1)

    def share(src, dst, send_sem, recv_sem, to):
        return pltpu.make_async_remote_copy(
            src_ref=src,
            dst_ref=dst,
            send_sem=send_sem,
            recv_sem=recv_sem,
            device_id={"feat": to},
            device_id_type=pl.DeviceIdType.MESH,
        )

    def scatter(o, start):
        to, source = other(o), other(n - o)
        copy = share(part_ref.at[to], recv.at[me], send1.at[to], recv1.at[me], to)
        if start:
            copy.start()
        else:
            copy.wait_send()
            share(part_ref.at[source], recv.at[source], send1.at[source], recv1.at[source], source).wait_recv()

    def gather(o, start):
        to, source = other(o), other(n - o)
        copy = share(out_ref.at[me], out_ref.at[me], send2.at[to], recv2.at[me], to)
        if start:
            copy.start()
        else:
            copy.wait_send()
            share(out_ref.at[source], out_ref.at[source], send2.at[source], recv2.at[source], source).wait_recv()

    def each(step, start):
        def body(o, carry):
            step(o, start)
            return carry

        lax.fori_loop(1, n, body, 0)

    each(scatter, True)
    each(scatter, False)
    recv[me] = part_ref[me]
    total = recv[0].astype(F32)
    for s in range(1, n):
        total = total + recv[s].astype(F32)
    out_ref[me] = total.astype(out_ref.dtype)
    each(gather, True)
    each(gather, False)


def sum_shares(parts, n):
    vmem = pl.BlockSpec(memory_space=pltpu.VMEM)
    return pl.pallas_call(
        functools.partial(sum_kernel, n),
        out_shape=jax.ShapeDtypeStruct(parts.shape, BF16),
        in_specs=[vmem],
        out_specs=vmem,
        scratch_shapes=[pltpu.VMEM(parts.shape, BF16)] + [pltpu.SemaphoreType.DMA((n,))] * 4,
        compiler_params=pltpu.CompilerParams(collective_id=0, has_side_effects=True),
    )(parts)


def per_device(x_acts, delta, pattern, row_signs, col_signs, cols):
    examples, tokens, width = x_acts.shape
    rows = delta.shape[2]
    sketch = cols.shape[0]
    n = lax.axis_size("feat")
    me = lax.axis_index("feat")
    row_sign = lax.dynamic_slice_in_dim(row_signs, me * rows, rows).astype(BF16)[None]
    bands = max(rows // BLK, 1)
    band = lax.dynamic_slice_in_dim(pattern, me * rows // BLK, bands, 0)
    factor = jnp.repeat(band, BLK, axis=1) * col_signs[None]
    col_factor = factor.astype(F32) / tokens
    parts = local_sketch(me[None], x_acts, delta, row_sign, col_factor, cols)
    shape = parts.shape
    total = sum_shares(parts.reshape(n, parts.size // n // LANES, LANES), n).reshape(shape)
    total = total.reshape(shape[0], CHUNK // LANES, examples, LANES).transpose(2, 0, 1, 3)
    return total.reshape(examples, sketch).astype(F32) / math.sqrt(sketch)


def solution(mesh):
    placed = (P("grp", None, None), P("grp", None, "feat"), P(), P(), P(), P())
    return jax.shard_map(
        per_device, mesh=mesh, in_specs=placed, out_specs=P("grp", None), check_vma=False
    )
```

time: 285 us -> 64.6 us (0.23)
  local copies, waits for them, and re-layouts: 123 us -> 3.07 us
  other arithmetic: 68.6 us -> 3.04 us
  Pallas kernels: 0 us -> 57.8 us
  matrix products: 57 us -> 0 us
  blocking collectives: 22 us -> 0 us
  starting transfers between devices: 9.77 us -> 0 us
  waiting for transfers between devices: 2.92 us -> 0 us
    pallas_call x0 -> x2, Pallas kernels: none -> 57.8 us  [the longest x1 41.3 us: local_sketch(): pl.pallas_call(functools.partial(sketch_kernel, bins, tiles), grid=(examp...]
    dot_general x4 -> x0, matrix products: 57 us -> none  [the longest x1 21.4 us: column_section(): jnp.einsum('erqk,qp->pker', section, hadamard(high_width), precision=lax....]
    gather x2 -> x0, local copies, waits for them, and re-layouts: 55.5 us -> none  [the longest x1 49.4 us: kept_entries(): picked = jnp.take(section, cols % width_in, axis=0)]
    unnamed x2 -> x0, other arithmetic: 43.8 us -> none
    unnamed x12 -> x7, local copies, waits for them, and re-layouts: 42.9 us -> 2.29 us
    all_gather x1 -> x0, blocking collectives: 22 us -> none  [per_device(): gathered = lax.all_gather(mine[None], 'feat', axis=0, tiled=True)]
    dot_general x1 -> x0, other arithmetic: 21.1 us -> none  [kept_entries(): jnp.einsum('ker,rk->ek', picked, weight, precision=lax.Precision.HIGHEST)]
    reshape x2 -> x1, local copies, waits for them, and re-layouts: 21.3 us -> 0.77 us  [local_sketch(): cols.reshape(sketch // TILE, TILE)]
  transfers between devices with their start and end apart: 3 -> 0, of which waited for: 2 -> 0; matrix products, arithmetic and copies ran while one was open for 32% -> 0% of each run, Pallas kernels for 0% -> 0%
where the time goes in v1:
time: 64.6 us; the launch traced here: 64 us
  Pallas kernels  57.8 us (89%)
  local copies, waits for them, and re-layouts  3.07 us (5%)
  other arithmetic  3.04 us (5%)
    pallas_call x1, Pallas kernels, local_sketch(): pl.pallas_call(functools.partial(sketch_kernel, bins, tiles), grid=(examp...  41.3 us
    pallas_call x1, Pallas kernels, sum_shares(): pl.pallas_call(functools.partial(sum_kernel, n), out_shape=jax.ShapeDtype...  16.5 us
    unnamed x7, local copies, waits for them, and re-layouts  2.29 us
    div x1, other arithmetic, per_device(): return total.reshape(examples, sketch).astype(F32) / math.sqrt(sketch)  1.51 us

profile of v1, /device:TPU:0, one launch (start us, length us, event | category | flops | bytes accessed | tf_op | source)
XLA Modules:
  0.0 64.0 jit_solution(7145209853006002203)
XLA Ops:
  0.0 0.0 copy-start
  0.0 0.8 %dynamic-slice_convert_fusion = bf16[256]{0:T(256)(128)(2,1)S(1)} fusion(s32[4096]{0:T(1024)} %param.9, s32[]{:T(128)S(6)} %select_n.11), kind=kLoop, calls=%fused_computation.5 | loop fusion | flops 256 | bytes 1540 | tf_op jit(solution)/shard_map/convert_element_type | solution.py:342
  0.8 0.0 copy-done
  0.8 0.1 broadcast_bitcast_fusion
  0.9 0.8 %fusion.1.cf_ref = f32[2,4096]{1,0:T(2,128)S(1)} fusion(s32[1,2,32,128]{3,2,1,0:T(8,128)S(1)} %broadcast_bitcast_fusion, s32[4096]{0:T(1024)} %param.10), kind=kLoop, calls=%fused_computation.3 | loop fusion | flops 24576 | bytes 81920 | tf_op jit(solution)/shard_map/div | solution.py:346
  1.6 0.8 %reshape.16.cols_ref = s32[32,256]{1,0:T(8,128)S(1)} reshape(s32[8192]{0:T(1024)} %param.11) | data formatting | bytes 65536 | tf_op jit(solution)/shard_map/reshape | solution.py:259
  2.4 0.0 copy-start.1
  2.4 1.6 %copy-done.1 = bf16[4,1024,256]{2,1,0:T(8,128)(2,1)S(1)} copy-done((bf16[4,1024,256]{2,1,0:T(8,128)(2,1)S(1)}, bf16[4,1024,256]{2,1,0:T(8,128)(2,1)}, u32[]{:S(2)}) %copy-start.1) | copy-done | bytes 2097176
  4.0 41.3 %shard_map.64.part_ref = bf16[16,16,128]{2,1,0:T(8,128)(2,1)S(1)} custom-call(s32[1]{0:T(128)} %bitcast.me_ref, bf16[4,1024,4096]{2,1,0:T(8,128)(2,1)} %x_ref.1, bf16[4,1024,256]{2,1,0:T(8,128)(2,1)S(1)} %copy-done.1, bf16[1,256]{1,0:T(2,128)(2,1)S(1)} %broadcast_in_dim.11.rs_ref, f32[2,4096]{1,0:T(2,128)S(1)} %fusion.1.cf_ref, s32[32,256]{1,0:T(8,128)S(1)} %reshape.16.cols_ref), custom_call_target="tpu_custom_call" | custom-call | flops 8589934592 | bytes 35651584 | tf_op jit(solution)/shard_map/pallas_call | solution.py:227
  45.3 0.0 copy-start.2
  45.3 0.6 copy-done.2
  46.0 16.5 %shard_map.65 = bf16[16,16,128]{2,1,0:T(8,128)(2,1)} custom-call(bf16[16,16,128]{2,1,0:T(8,128)(2,1)} %copy-done.2), custom_call_target="tpu_custom_call" | custom-call | tf_op jit(solution)/shard_map/pallas_call | solution.py:326
  62.5 1.5 %convert_multiply_fusion = f32[16,16,128]{2,1,0:T(8,128)} fusion(bf16[16,16,128]{2,1,0:T(8,128)(2,1)} %shard_map.65), kind=kLoop, calls=%fused_computation | loop fusion | flops 65536 | bytes 196608 | tf_op jit(solution)/shard_map/div | solution.py:351
  (2 shorter events, 0.0 us)
Async XLA Ops:
  0.0 0.8 %copy-start = (s32[32,32]{1,0:T(8,128)S(1)}, s32[32,32]{1,0:T(8,128)}, u32[]{:S(2)}) copy-start(s32[32,32]{1,0:T(8,128)} %param.8) | copy-start | bytes 12292
  2.4 1.6 %copy-start.1 = (bf16[4,1024,256]{2,1,0:T(8,128)(2,1)S(1)}, bf16[4,1024,256]{2,1,0:T(8,128)(2,1)}, u32[]{:S(2)}) copy-start(bf16[4,1024,256]{2,1,0:T(8,128)(2,1)} %delta_ref.1) | copy-start | bytes 6291460
  45.3 0.6 copy-start.2

commit v2 on v1

v2 whole, which is shorter than its diff:
```python
import functools
import math

import jax
import jax.numpy as jnp
from jax import lax
from jax.experimental import pallas as pl
from jax.experimental.pallas import tpu as pltpu
from jax.sharding import PartitionSpec as P

BLK = 128
LANES = 128
TILE = 256
CHUNK = 512
F32 = jnp.float32
BF16 = jnp.bfloat16
NT = (((1,), (1,)), ((), ()))


def parity(value, bits):
    shift = 1
    while shift < bits:
        shift *= 2
    while shift > 1:
        shift //= 2
        value = value ^ (value >> shift)
    return value & 1


def sign_of(left, right, bits):
    return (1 - 2 * parity(left & right, bits)).astype(F32)


def iota(shape, axis):
    return lax.broadcasted_iota(jnp.int32, shape, axis)


def hits(cols_ref, a, bins, width):
    block = (cols_ref[:, pl.ds(pl.multiple_of(a * TILE, TILE), TILE)] % width) // LANES
    return iota((bins, TILE), 0) == block


def count(cols_ref, rank_ref, start_ref, info_v, bins, width):
    n_rows = cols_ref.shape[1] // TILE
    before = (iota((TILE, 2 * TILE), 0) < iota((TILE, 2 * TILE), 1)).astype(F32).astype(BF16)
    hit = [hits(cols_ref, a, bins, width).astype(F32) for a in range(n_rows)]
    ahead = jnp.dot(
        jnp.concatenate(hit, axis=0).astype(BF16), before, preferred_element_type=F32
    )
    running = jnp.zeros((bins, TILE), F32)
    for a in range(n_rows):
        here = ahead[a * bins : (a + 1) * bins]
        rank = jnp.sum(hit[a] * (here[:, :TILE] + running), axis=0, keepdims=True)
        rank_ref[a : a + 1, :] = rank.astype(jnp.int32)
        running = running + here[:, TILE:]
    need = (running.astype(jnp.int32) + (TILE - 1)) // TILE
    lower = (iota((bins, bins), 1) < iota((bins, bins), 0)).astype(F32).astype(BF16)
    start = jnp.dot(lower, need.astype(F32).astype(BF16), preferred_element_type=F32)
    start_ref[...] = start
    ends = start.astype(jnp.int32) + need
    tile_ids = iota((bins, LANES), 1)
    owner = jnp.sum((ends[:, :LANES] <= tile_ids).astype(jnp.int32), axis=0, keepdims=True)
    owner = jnp.minimum(owner, bins - 1)
    used = ends[bins - 1 :, :LANES]
    info_v[...] = jnp.where(iota((8, LANES), 0) == 0, owner, used)


def place(a, cols_ref, rank_ref, start_ref, tp_ref, lp_ref, bins, width, rows, tiles):
    slots = 2 * tiles
    first = jnp.sum(
        jnp.where(hits(cols_ref, a, bins, width), start_ref[...], 0.0), axis=0, keepdims=True
    )
    rank = rank_ref[pl.ds(a, 1), :]
    lane = rank % TILE
    slot = first.astype(jnp.int32) + rank // TILE + (lane // LANES) * tiles
    lane = lane % LANES
    tp_ref[pl.ds(a, 1), :] = slot
    lp_ref[pl.ds(a, 1), :] = lane
    cols = cols_ref[:, pl.ds(pl.multiple_of(a * TILE, TILE), TILE)]
    row = ((cols // width) % rows).astype(F32)
    col = (cols % LANES).astype(F32)
    here = iota((slots, TILE), 0) == slot
    left = jnp.concatenate([jnp.where(here, row, 0.0), jnp.where(here, col, 0.0)], axis=0)
    right = (iota((LANES, TILE), 0) == lane).astype(F32)
    return lax.dot_general(
        left.astype(BF16), right.astype(BF16), NT, preferred_element_type=F32
    )


def stages(parts, first, last):
    half = first
    while half < last:
        for c in range(len(parts)):
            if not c & half:
                low, high = parts[c], parts[c + half]
                parts[c], parts[c + half] = low + high, low - high
        half *= 2
    return parts


def butterfly(g_ref, t1_ref, work_ref, slot, e, step, steps):
    bins, lanes, rows = g_ref.shape[1:]
    share = lanes // steps
    wide = min(rows, LANES)
    unit = 0
    for j in range(share // 16):
        at = pl.ds(pl.multiple_of(step * share + j * 16, 16), 16)
        for h in range(rows // wide):
            span = slice(h * wide, (h + 1) * wide)
            inner = 8 if bins % 8 == 0 else bins
            for c0 in range(0, bins, inner):
                parts = [g_ref[slot, c0 + c, at, span].astype(F32) for c in range(inner)]
                for c, part in enumerate(stages(parts, 1, inner)):
                    work_ref[unit, c0 + c] = part
            for c0 in range(inner):
                parts = [work_ref[unit, c] for c in range(c0, bins, inner)]
                for c, part in enumerate(stages(parts, 1, len(parts))):
                    t1_ref[c0 + c * inner, e, at, span] = part.astype(BF16)
            unit += 1


def tile_values(t, rc_ref, info_s, t1_ref, so_ref):
    examples, _, rows = t1_ref.shape[1:]
    row = rc_ref[0, pl.ds(t, 1), :]
    col = rc_ref[1, pl.ds(t, 1), :]
    low_ids = iota((16, TILE), 0)
    row_low = sign_of(low_ids, row % 16, 4).astype(BF16)
    high_bits = rows // 16
    row_high = sign_of(iota((max(high_bits, 8), TILE), 0), row // 16, 8).astype(BF16)
    weight = jnp.concatenate([row_low * row_high[h : h + 1] for h in range(high_bits)], axis=0)
    block = t1_ref[info_s[0, t]].reshape(examples * LANES, rows)
    value = jnp.dot(block, weight, preferred_element_type=F32)
    col_low = sign_of(iota((8, TILE), 0), col % 8, 3)
    col_high = sign_of(iota((16, TILE), 0), col // 8, 4)
    for e in range(examples):
        total = jnp.zeros((8, TILE), F32)
        for h in range(16):
            at = e * LANES + h * 8
            total = total + value[at : at + 8] * col_high[h : h + 1]
        so_ref[e, pl.ds(t, 1), :] = jnp.sum(total * col_low, axis=0, keepdims=True)


def entries(a, me, table_ref, tp_ref, lp_ref, cols_ref, n_examples, chunk, width, rows):
    per = chunk // TILE

    def wide(ref):
        return jnp.concatenate([ref[pl.ds(per * a + u, 1), :] for u in range(per)], axis=1)

    pick = (iota((table_ref.shape[1], chunk), 0) == wide(tp_ref)).astype(F32).astype(BF16)
    spread = jnp.dot(table_ref[...], pick, preferred_element_type=F32)
    mine = iota((LANES, chunk), 0) == wide(lp_ref)
    high = cols_ref[:, pl.ds(pl.multiple_of(a * chunk, chunk), chunk)] // (width * rows)
    sign = sign_of(high, me, 16)
    kept = [
        jnp.sum(jnp.where(mine, spread[e * LANES : (e + 1) * LANES], 0.0), axis=0, keepdims=True)
        * sign
        for e in range(n_examples)
    ]
    lines = [
        kept[e][:, q * LANES : (q + 1) * LANES]
        for q in range(chunk // LANES)
        for e in range(n_examples)
    ]
    return jnp.concatenate(lines, axis=0).astype(BF16)


def sketch_kernel(
    tiles, me_ref, x_ref, delta_ref, pattern_ref, rs_ref, cs_ref, cols_ref, table_ref, tp_ref, lp_ref,
    dt_ref, cf_ref, g_ref, t1_ref, work_ref, rank_ref, start_ref, pacc_ref, rc_ref, so_ref,
    info_v, info_s, sem,
):
    e, nb = pl.program_id(0), pl.program_id(1)
    examples, steps = pl.num_programs(0), pl.num_programs(1)
    bins, lanes, rows = g_ref.shape[1:]
    n_examples, n_steps = t1_ref.shape[1], cf_ref.shape[0]
    width = bins * lanes
    tokens, step_cols = x_ref.shape[1:]
    bands = cf_ref.shape[1]
    step_blocks = step_cols // LANES
    step = e * n_steps + nb
    n_rows = rank_ref.shape[0]
    me = me_ref[0]

    @pl.when(step == 0)
    def _():
        count(cols_ref, rank_ref, start_ref, info_v, bins, width)
        copy = pltpu.make_async_copy(info_v, info_s, sem)
        copy.start()
        pacc_ref[...] = jnp.zeros_like(pacc_ref)
        so_ref[...] = jnp.zeros_like(so_ref)
        for b in range(bands):
            band = pattern_ref[pl.ds(me * rows // BLK + b, 1), :]
            for c in range(width // BLK):
                at = (c * BLK) % step_cols
                factor = band[:, c : c + 1] * cs_ref[:, c * BLK : (c + 1) * BLK]
                cf_ref[c * BLK // step_cols, b : b + 1, at : at + BLK] = factor.astype(F32) / tokens
        copy.wait()

    @pl.when(nb == 0)
    def _():
        span = max(rows, LANES)
        window = rs_ref[:, pl.ds(pl.multiple_of(me * rows // span * span, span), span)]
        own = window[:, :rows]
        for u in range(1, span // rows):
            own = jnp.where(me % (span // rows) == u, window[:, u * rows : (u + 1) * rows], own)
        dt_ref[...] = (delta_ref[0] * own.astype(F32).astype(BF16)).T

    slot = lax.rem(e, 2)
    last = lax.rem(e + n_examples - 1, n_examples)
    butterfly(g_ref, t1_ref, work_ref, 1 - slot, last, nb, n_steps)

    per_step = -(-n_rows // (n_examples * n_steps))
    for u in range(per_step):
        pacc_ref[...] += place(
            step * per_step + u, cols_ref, rank_ref, start_ref, tp_ref, lp_ref, bins, width, rows, tiles
        )

    acc = jnp.dot(dt_ref[...], x_ref[0], preferred_element_type=F32)
    per = min(rows, BLK)
    factor = cf_ref[nb]
    for c in range(step_blocks):
        span = slice(c * LANES, (c + 1) * LANES)
        block = [
            (acc[b * per : (b + 1) * per, span] * factor[b : b + 1, span]).astype(BF16)
            for b in range(rows // per)
        ]
        g_ref[slot, nb * step_blocks + c] = jnp.concatenate(block, axis=0).T

    @pl.when(step == examples * steps - 1)
    def _():
        for q in range(n_steps):
            butterfly(g_ref, t1_ref, work_ref, slot, e, q, n_steps)
        for v in range(2):
            part = pacc_ref[2 * tiles * v : 2 * tiles * (v + 1)].astype(jnp.int32)
            rc_ref[v] = jnp.concatenate([part[:tiles], part[tiles:]], axis=1)

        def four(s, carry):
            for u in range(4):
                tile_values(s * 4 + u, rc_ref, info_s, t1_ref, so_ref)
            return carry

        lax.fori_loop(0, (info_s[1, 0] + 3) // 4, four, 0)
        for k in range(n_examples):
            one = so_ref[k]
            both = jnp.concatenate([one[:, :LANES], one[:, LANES:]], axis=0)
            table_ref[k * LANES : (k + 1) * LANES] = both.T.astype(BF16)


def local_sketch(me, x_acts, delta, pattern, row_signs, col_signs, cols):
    examples, tokens, width = x_acts.shape
    rows = delta.shape[2]
    sketch = cols.shape[1]
    bins = width // LANES
    tiles = sketch // TILE + bins
    step_cols = 1024
    steps = width // step_cols
    n_rows = sketch // TILE
    bands = max(rows // BLK, 1)
    smem = pl.BlockSpec(memory_space=pltpu.SMEM)
    whole = lambda shape: pl.BlockSpec(shape, lambda e, n: (0,) * len(shape))
    units = LANES // steps // 16 * max(rows // LANES, 1)
    table = (examples * LANES, 2 * tiles)
    places = (n_rows, TILE)
    return pl.pallas_call(
        functools.partial(sketch_kernel, tiles),
        grid=(examples, steps),
        out_shape=[
            jax.ShapeDtypeStruct(table, BF16),
            jax.ShapeDtypeStruct(places, jnp.int32),
            jax.ShapeDtypeStruct(places, jnp.int32),
        ],
        in_specs=[
            smem,
            pl.BlockSpec((1, tokens, step_cols), lambda e, n: (e, 0, n)),
            pl.BlockSpec((1, tokens, rows), lambda e, n: (e, 0, 0)),
            whole(pattern.shape),
            whole(row_signs.shape),
            whole(col_signs.shape),
            whole(cols.shape),
        ],
        out_specs=[whole(table), whole(places), whole(places)],
        scratch_shapes=[
            pltpu.VMEM((rows, tokens), BF16),
            pltpu.VMEM((steps, bands, step_cols), F32),
            pltpu.VMEM((2, bins, LANES, rows), BF16),
            pltpu.VMEM((bins, examples, LANES, rows), BF16),
            pltpu.VMEM((units, bins, 16, min(rows, LANES)), F32),
            pltpu.VMEM(places, jnp.int32),
            pltpu.VMEM((bins, TILE), F32),
            pltpu.VMEM((4 * tiles, LANES), F32),
            pltpu.VMEM((2, tiles, TILE), jnp.int32),
            pltpu.VMEM((examples, tiles, TILE), F32),
            pltpu.VMEM((8, LANES), jnp.int32),
            pltpu.SMEM((8, LANES), jnp.int32),
            pltpu.SemaphoreType.DMA,
        ],
        compiler_params=pltpu.CompilerParams(vmem_limit_bytes=60 * 2**20),
        cost_estimate=pl.CostEstimate(
            flops=2 * examples * tokens * width * rows,
            bytes_accessed=2 * examples * tokens * (width + rows),
            transcendentals=0,
        ),
    )(me, x_acts, delta, pattern, row_signs, col_signs, cols)


def sum_kernel(
    n, n_examples, chunk, width, rows, table_ref, tp_ref, lp_ref, cols_ref, out_ref,
    part, recv, send1, recv1, send2, recv2,
):
    me = lax.axis_index("feat")
    chunks = cols_ref.shape[1] // chunk
    pieces = n // chunks
    lines = part.shape[1]
    barrier = pltpu.get_barrier_semaphore()

    def other(o):
        return lax.rem(me + o, n)

    def loop(first, last, step):
        def body(o, carry):
            step(o)
            return carry

        lax.fori_loop(first, last, body, 0)

    def greet(o):
        pl.semaphore_signal(
            barrier, inc=1, device_id={"feat": other(o)}, device_id_type=pl.DeviceIdType.MESH
        )

    def share(src, dst, send_sem, recv_sem, to):
        return pltpu.make_async_remote_copy(
            src_ref=src,
            dst_ref=dst,
            send_sem=send_sem,
            recv_sem=recv_sem,
            device_id={"feat": to},
            device_id_type=pl.DeviceIdType.MESH,
        )

    def chunk_at(o):
        return lax.rem(me // pieces + 1 + o, chunks)

    def compute(o):
        a = chunk_at(o)
        found = entries(
            a, me, table_ref, tp_ref, lp_ref, cols_ref, n_examples, chunk, width, rows
        )
        for p in range(pieces):
            part[a * pieces + p] = found[p * lines : (p + 1) * lines]

    def send(o):
        for p in range(pieces):
            to = chunk_at(o) * pieces + p

            @pl.when(to != me)
            def _():
                share(part.at[to], recv.at[me], send1.at[to], recv1.at[me], to).start()

    def step(o):
        compute(o)
        send(o)

    loop(1, n, greet)
    compute(0)
    pl.semaphore_wait(barrier, n - 1)
    send(0)
    loop(1, chunks, step)

    def collect(o, total):
        source = other(n - o)
        share(part.at[source], recv.at[source], send1.at[source], recv1.at[source], source).wait_recv()
        return total + recv[source].astype(F32)

    out_ref[me] = lax.fori_loop(1, n, collect, part[me].astype(F32))

    def spread(o):
        to = other(o)
        share(out_ref.at[me], out_ref.at[me], send2.at[to], recv2.at[me], to).start()

    loop(1, n, spread)

    def finish(o):
        to, source = other(o), other(n - o)
        share(part.at[to], recv.at[me], send1.at[to], recv1.at[me], to).wait_send()
        share(out_ref.at[me], out_ref.at[me], send2.at[to], recv2.at[me], to).wait_send()
        share(out_ref.at[source], out_ref.at[source], send2.at[source], recv2.at[source], source).wait_recv()

    loop(1, n, finish)


def sum_shares(table, slots, places, cols, n, examples, chunk, width, rows):
    vmem = pl.BlockSpec(memory_space=pltpu.VMEM)
    shape = (n, cols.shape[1] // n * examples // LANES, LANES)
    return pl.pallas_call(
        functools.partial(sum_kernel, n, examples, chunk, width, rows),
        out_shape=jax.ShapeDtypeStruct(shape, F32),
        in_specs=[vmem] * 4,
        out_specs=vmem,
        scratch_shapes=[pltpu.VMEM(shape, BF16)] * 2 + [pltpu.SemaphoreType.DMA((n,))] * 4,
        compiler_params=pltpu.CompilerParams(
            collective_id=0, has_side_effects=True, vmem_limit_bytes=32 * 2**20
        ),
    )(table, slots, places, cols)


def per_device(x_acts, delta, pattern, row_signs, col_signs, cols):
    examples, tokens, width = x_acts.shape
    rows = delta.shape[2]
    sketch = cols.shape[0]
    n = lax.axis_size("feat")
    me = lax.axis_index("feat")
    chunk = max(sketch // n, CHUNK)
    cols = cols[None]
    table, slots, places = local_sketch(
        me[None], x_acts, delta, pattern, row_signs[None], col_signs[None], cols
    )
    total = sum_shares(table, slots, places, cols, n, examples, chunk, width, rows)
    total = total.reshape(sketch // chunk, chunk // LANES, examples, LANES).transpose(2, 0, 1, 3)
    return total.reshape(examples, sketch) / math.sqrt(sketch)


def solution(mesh):
    placed = (P("grp", None, None), P("grp", None, "feat"), P(), P(), P(), P())
    return jax.shard_map(
        per_device, mesh=mesh, in_specs=placed, out_specs=P("grp", None), check_vma=False
    )
```

time: 64.6 us -> 56.4 us (0.87)
  Pallas kernels: 57.8 us -> 53 us
  other arithmetic: 3.04 us -> 0.67 us
  local copies, waits for them, and re-layouts: 3.07 us -> 2.42 us
    pallas_call x2, Pallas kernels: 57.8 us -> 53 us  [the longest x1 34.3 us: local_sketch(): pl.pallas_call(functools.partial(sketch_kernel, tiles), grid=(examples, s...]
    div x2 -> x1, other arithmetic: 2.26 us -> 0.67 us  [per_device(): return total.reshape(examples, sketch) / math.sqrt(sketch)]
    convert_element_type x1 -> x0, other arithmetic: 0.77 us -> none  [per_device(): lax.dynamic_slice_in_dim(row_signs, me * rows, rows).astype(BF16)[None]]
    reshape x1 -> x0, local copies, waits for them, and re-layouts: 0.77 us -> none  [local_sketch(): cols.reshape(sketch // TILE, TILE)]
    unnamed x7 -> x8, local copies, waits for them, and re-layouts: 2.29 us -> 2.42 us
where the time goes in v2:
time: 56.4 us; the launch traced here: 56.1 us
  Pallas kernels  53 us (94%)
  local copies, waits for them, and re-layouts  2.42 us (4%)
  other arithmetic  0.67 us (1%)
    pallas_call x1, Pallas kernels, local_sketch(): pl.pallas_call(functools.partial(sketch_kernel, tiles), grid=(examples, s...  34.3 us
    pallas_call x1, Pallas kernels, sum_shares(): pl.pallas_call(functools.partial(sum_kernel, n, examples, chunk, width, r...  18.7 us
    unnamed x8, local copies, waits for them, and re-layouts  2.42 us

profile of v2, /device:TPU:0, one launch (start us, length us, event | category | flops | bytes accessed | tf_op | source)
XLA Modules:
  0.0 56.1 jit_solution(12192885151807078448)
XLA Ops:
  0.0 0.0 copy-start.1
  0.0 34.3 %shard_map.64 = (bf16[512,128]{1,0:T(8,128)(2,1)}, s32[32,256]{1,0:T(8,128)}, s32[32,256]{1,0:T(8,128)}) custom-call(s32[1]{0:T(128)} %bitcast.me_ref, bf16[4,1024,4096]{2,1,0:T(8,128)(2,1)} %x_ref.1, bf16[4,1024,256]{2,1,0:T(8,128)(2,1)} %delta_ref.1, s32[32,32]{1,0:T(8,128)} %pattern_ref.1, s32[1,4096]{1,0:T(1,128)} %bitcast.11, s32[1,4096]{1,0:T(1,128)} %bitcast.12, ...), custom_call_target="tpu_custom_call" | custom-call | flops 8589934592 | bytes 35651584 | tf_op jit(solution)/shard_map/pallas_call | solution.py:264
  34.3 0.0 copy-done.1
  34.3 0.0 copy-start
  34.3 0.9 %copy-done = bf16[512,128]{1,0:T(8,128)(2,1)S(1)} copy-done((bf16[512,128]{1,0:T(8,128)(2,1)S(1)}, bf16[512,128]{1,0:T(8,128)(2,1)}, u32[]{:S(2)}) %copy-start) | copy-done | bytes 131096
  35.2 0.0 copy-start.2
  35.2 0.8 %copy-done.2 = s32[32,256]{1,0:T(8,128)S(1)} copy-done((s32[32,256]{1,0:T(8,128)S(1)}, s32[32,256]{1,0:T(8,128)}, u32[]{:S(2)}) %copy-start.2) | copy-done | bytes 32792
  36.0 0.0 copy-start.3
  36.0 0.8 %copy-done.3 = s32[32,256]{1,0:T(8,128)S(1)} copy-done((s32[32,256]{1,0:T(8,128)S(1)}, s32[32,256]{1,0:T(8,128)}, u32[]{:S(2)}) %copy-start.3) | copy-done | bytes 32792
  36.7 18.7 %shard_map.65 = f32[16,16,128]{2,1,0:T(8,128)S(1)} custom-call(bf16[512,128]{1,0:T(8,128)(2,1)S(1)} %copy-done, s32[32,256]{1,0:T(8,128)S(1)} %copy-done.2, s32[32,256]{1,0:T(8,128)S(1)} %copy-done.3, s32[1,8192]{1,0:T(1,128)S(1)} %bitcast.10), custom_call_target="tpu_custom_call" | custom-call | tf_op jit(solution)/shard_map/pallas_call | solution.py:395
  55.5 0.7 %broadcast_multiply_fusion = f32[16,16,128]{2,1,0:T(8,128)} fusion(f32[16,16,128]{2,1,0:T(8,128)S(1)} %shard_map.65), kind=kLoop, calls=%fused_computation | loop fusion | flops 32768 | bytes 262144 | tf_op jit(solution)/shard_map/div | solution.py:420
Async XLA Ops:
  0.0 34.3 %copy-start.1 = (s32[8192]{0:T(1024)S(1)}, s32[8192]{0:T(1024)}, u32[]{:S(2)}) copy-start(s32[8192]{0:T(1024)} %param.11) | copy-start | bytes 98308
  34.3 0.9 %copy-start = (bf16[512,128]{1,0:T(8,128)(2,1)S(1)}, bf16[512,128]{1,0:T(8,128)(2,1)}, u32[]{:S(2)}) copy-start(bf16[512,128]{1,0:T(8,128)(2,1)} %get-tuple-element.8.table_ref) | copy-start | bytes 393220
  35.2 0.8 %copy-start.2 = (s32[32,256]{1,0:T(8,128)S(1)}, s32[32,256]{1,0:T(8,128)}, u32[]{:S(2)}) copy-start(s32[32,256]{1,0:T(8,128)} %get-tuple-element.9.tp_ref) | copy-start | bytes 98308
  36.0 0.8 %copy-start.3 = (s32[32,256]{1,0:T(8,128)S(1)}, s32[32,256]{1,0:T(8,128)}, u32[]{:S(2)}) copy-start(s32[32,256]{1,0:T(8,128)} %get-tuple-element.10.lp_ref) | copy-start | bytes 98308

commit v3 on v2

--- a/solution.py
+++ b/solution.py
@@ -15,6 +15,7 @@
 F32 = jnp.float32
 BF16 = jnp.bfloat16
 NT = (((1,), (1,)), ((), ()))
+TN = (((0,), (0,)), ((), ()))
 
 
 def parity(value, bits):
@@ -165,18 +166,20 @@
 
 
 def sketch_kernel(
-    tiles, me_ref, x_ref, delta_ref, pattern_ref, rs_ref, cs_ref, cols_ref, table_ref, tp_ref, lp_ref,
-    dt_ref, cf_ref, g_ref, t1_ref, work_ref, rank_ref, start_ref, pacc_ref, rc_ref, so_ref,
-    info_v, info_s, sem,
+    tiles, me_ref, x_ref, delta_ref, pattern_ref, rs_ref, cs_ref, cols_ref, table_out, tp_out, lp_out,
+    table_ref, tp_ref, lp_ref, dt_ref, cf_ref, g_ref, t1_ref, work_ref, rank_ref, start_ref, pacc_ref, rc_ref, so_ref,
+    info_v, info_s, sem, out_sem,
 ):
     e, nb = pl.program_id(0), pl.program_id(1)
     examples, steps = pl.num_programs(0), pl.num_programs(1)
     bins, lanes, rows = g_ref.shape[1:]
-    n_examples, n_steps = t1_ref.shape[1], cf_ref.shape[0]
+    n_examples = t1_ref.shape[1]
     width = bins * lanes
     tokens, step_cols = x_ref.shape[1:]
-    bands = cf_ref.shape[1]
-    step_blocks = step_cols // LANES
+    n_steps = width // step_cols
+    per = min(rows, BLK)
+    bands = rows // per
+    step_blocks = step_cols // lanes
     step = e * n_steps + nb
     n_rows = rank_ref.shape[0]
     me = me_ref[0]
@@ -190,10 +193,10 @@
         so_ref[...] = jnp.zeros_like(so_ref)
         for b in range(bands):
             band = pattern_ref[pl.ds(me * rows // BLK + b, 1), :]
-            for c in range(width // BLK):
-                at = (c * BLK) % step_cols
-                factor = band[:, c : c + 1] * cs_ref[:, c * BLK : (c + 1) * BLK]
-                cf_ref[c * BLK // step_cols, b : b + 1, at : at + BLK] = factor.astype(F32) / tokens
+            for c in range(bins):
+                factor = band[:, c : c + 1] * cs_ref[:, c * lanes : (c + 1) * lanes]
+                factor = jnp.broadcast_to(factor.astype(F32) / tokens, (per, lanes))
+                cf_ref[c, :, b * per : (b + 1) * per] = factor.T
         copy.wait()
 
     @pl.when(nb == 0)
@@ -203,7 +206,7 @@
         own = window[:, :rows]
         for u in range(1, span // rows):
             own = jnp.where(me % (span // rows) == u, window[:, u * rows : (u + 1) * rows], own)
-        dt_ref[...] = (delta_ref[0] * own.astype(F32).astype(BF16)).T
+        dt_ref[...] = delta_ref[0] * own.astype(F32).astype(BF16)
 
     slot = lax.rem(e, 2)
     last = lax.rem(e + n_examples - 1, n_examples)
@@ -215,19 +218,17 @@
             step * per_step + u, cols_ref, rank_ref, start_ref, tp_ref, lp_ref, bins, width, rows, tiles
         )
 
-    acc = jnp.dot(dt_ref[...], x_ref[0], preferred_element_type=F32)
-    per = min(rows, BLK)
-    factor = cf_ref[nb]
+    acc = lax.dot_general(x_ref[0], dt_ref[...], TN, preferred_element_type=F32)
     for c in range(step_blocks):
-        span = slice(c * LANES, (c + 1) * LANES)
-        block = [
-            (acc[b * per : (b + 1) * per, span] * factor[b : b + 1, span]).astype(BF16)
-            for b in range(rows // per)
-        ]
-        g_ref[slot, nb * step_blocks + c] = jnp.concatenate(block, axis=0).T
+        block = acc[c * lanes : (c + 1) * lanes] * cf_ref[nb * step_blocks + c]
+        g_ref[slot, nb * step_blocks + c] = block.astype(BF16)
 
     @pl.when(step == examples * steps - 1)
     def _():
+        slots_out = pltpu.make_async_copy(tp_ref, tp_out, out_sem.at[0])
+        lanes_out = pltpu.make_async_copy(lp_ref, lp_out, out_sem.at[1])
+        slots_out.start()
+        lanes_out.start()
         for q in range(n_steps):
             butterfly(g_ref, t1_ref, work_ref, slot, e, q, n_steps)
         for v in range(2):
@@ -244,6 +245,11 @@
             one = so_ref[k]
             both = jnp.concatenate([one[:, :LANES], one[:, LANES:]], axis=0)
             table_ref[k * LANES : (k + 1) * LANES] = both.T.astype(BF16)
+        table_copy = pltpu.make_async_copy(table_ref, table_out, out_sem.at[2])
+        table_copy.start()
+        slots_out.wait()
+        lanes_out.wait()
+        table_copy.wait()
 
 
 def local_sketch(me, x_acts, delta, pattern, row_signs, col_signs, cols):
@@ -255,7 +261,6 @@
     step_cols = 1024
     steps = width // step_cols
     n_rows = sketch // TILE
-    bands = max(rows // BLK, 1)
     smem = pl.BlockSpec(memory_space=pltpu.SMEM)
     whole = lambda shape: pl.BlockSpec(shape, lambda e, n: (0,) * len(shape))
     units = LANES // steps // 16 * max(rows // LANES, 1)
@@ -278,10 +283,13 @@
             whole(col_signs.shape),
             whole(cols.shape),
         ],
-        out_specs=[whole(table), whole(places), whole(places)],
+        out_specs=[pl.BlockSpec(memory_space=pltpu.HBM)] * 3,
         scratch_shapes=[
-            pltpu.VMEM((rows, tokens), BF16),
-            pltpu.VMEM((steps, bands, step_cols), F32),
+            pltpu.VMEM(table, BF16),
+            pltpu.VMEM(places, jnp.int32),
+            pltpu.VMEM(places, jnp.int32),
+            pltpu.VMEM((tokens, rows), BF16),
+            pltpu.VMEM((bins, LANES, rows), F32),
             pltpu.VMEM((2, bins, LANES, rows), BF16),
             pltpu.VMEM((bins, examples, LANES, rows), BF16),
             pltpu.VMEM((units, bins, 16, min(rows, LANES)), F32),
@@ -293,6 +301,7 @@
             pltpu.VMEM((8, LANES), jnp.int32),
             pltpu.SMEM((8, LANES), jnp.int32),
             pltpu.SemaphoreType.DMA,
+            pltpu.SemaphoreType.DMA((3,)),
         ],
         compiler_params=pltpu.CompilerParams(vmem_limit_bytes=60 * 2**20),
         cost_estimate=pl.CostEstimate(
@@ -358,14 +367,18 @@
                 share(part.at[to], recv.at[me], send1.at[to], recv1.at[me], to).start()
 
     def step(o):
-        compute(o)
-        send(o)
+        compute(2 * o)
+        compute(2 * o + 1)
+        send(2 * o)
+        send(2 * o + 1)
 
     loop(1, n, greet)
     compute(0)
+    compute(1)
     pl.semaphore_wait(barrier, n - 1)
     send(0)
-    loop(1, chunks, step)
+    send(1)
+    loop(1, chunks // 2, step)
 
     def collect(o, total):
         source = other(n - o)

time: 56.4 us -> 54.3 us (0.963)
  Pallas kernels: 53 us -> 50.9 us
    pallas_call x1, Pallas kernels: 18.7 us -> 17.4 us  [sum_shares(): pl.pallas_call(functools.partial(sum_kernel, n, examples, chunk, width, r...]
    pallas_call x1, Pallas kernels: 34.3 us -> 33.5 us  [local_sketch(): pl.pallas_call(functools.partial(sketch_kernel, tiles), grid=(examples, s...]
where the time goes in v3:
time: 54.3 us; the launch traced here: 54 us
  Pallas kernels  50.9 us (94%)
  local copies, waits for them, and re-layouts  2.42 us (4%)
  other arithmetic  0.67 us (1%)
    pallas_call x1, Pallas kernels, local_sketch(): pl.pallas_call(functools.partial(sketch_kernel, tiles), grid=(examples, s...  33.5 us
    pallas_call x1, Pallas kernels, sum_shares(): pl.pallas_call(functools.partial(sum_kernel, n, examples, chunk, width, r...  17.4 us
    unnamed x8, local copies, waits for them, and re-layouts  2.42 us

profile of v3, /device:TPU:0, one launch (start us, length us, event | category | flops | bytes accessed | tf_op | source)
XLA Modules:
  0.0 54.0 jit_solution(8065571342135253645)
XLA Ops:
  0.0 0.0 copy-start.1
  0.0 33.5 %shard_map.64 = (bf16[512,128]{1,0:T(8,128)(2,1)}, s32[32,256]{1,0:T(8,128)}, s32[32,256]{1,0:T(8,128)}) custom-call(s32[1]{0:T(128)} %bitcast.me_ref, bf16[4,1024,4096]{2,1,0:T(8,128)(2,1)} %x_ref.1, bf16[4,1024,256]{2,1,0:T(8,128)(2,1)} %delta_ref.1, s32[32,32]{1,0:T(8,128)} %pattern_ref.1, s32[1,4096]{1,0:T(1,128)} %bitcast.11, s32[1,4096]{1,0:T(1,128)} %bitcast.12, ...), custom_call_target="tpu_custom_call" | custom-call | flops 8589934592 | bytes 35651584 | tf_op jit(solution)/shard_map/pallas_call | solution.py:269
  33.5 0.0 copy-done.1
  33.5 0.0 copy-start
  33.5 0.9 %copy-done = bf16[512,128]{1,0:T(8,128)(2,1)S(1)} copy-done((bf16[512,128]{1,0:T(8,128)(2,1)S(1)}, bf16[512,128]{1,0:T(8,128)(2,1)}, u32[]{:S(2)}) %copy-start) | copy-done | bytes 131096
  34.4 0.0 copy-start.2
  34.4 0.8 %copy-done.2 = s32[32,256]{1,0:T(8,128)S(1)} copy-done((s32[32,256]{1,0:T(8,128)S(1)}, s32[32,256]{1,0:T(8,128)}, u32[]{:S(2)}) %copy-start.2) | copy-done | bytes 32792
  35.2 0.0 copy-start.3
  35.2 0.8 %copy-done.3 = s32[32,256]{1,0:T(8,128)S(1)} copy-done((s32[32,256]{1,0:T(8,128)S(1)}, s32[32,256]{1,0:T(8,128)}, u32[]{:S(2)}) %copy-start.3) | copy-done | bytes 32792
  35.9 17.4 %shard_map.65 = f32[16,16,128]{2,1,0:T(8,128)S(1)} custom-call(bf16[512,128]{1,0:T(8,128)(2,1)S(1)} %copy-done, s32[32,256]{1,0:T(8,128)S(1)} %copy-done.2, s32[32,256]{1,0:T(8,128)S(1)} %copy-done.3, s32[1,8192]{1,0:T(1,128)S(1)} %bitcast.10), custom_call_target="tpu_custom_call" | custom-call | tf_op jit(solution)/shard_map/pallas_call | solution.py:408
  53.4 0.7 %broadcast_multiply_fusion = f32[16,16,128]{2,1,0:T(8,128)} fusion(f32[16,16,128]{2,1,0:T(8,128)S(1)} %shard_map.65), kind=kLoop, calls=%fused_computation | loop fusion | flops 32768 | bytes 262144 | tf_op jit(solution)/shard_map/div | solution.py:433
Async XLA Ops:
  0.0 33.5 %copy-start.1 = (s32[8192]{0:T(1024)S(1)}, s32[8192]{0:T(1024)}, u32[]{:S(2)}) copy-start(s32[8192]{0:T(1024)} %param.11) | copy-start | bytes 98308
  33.5 0.9 %copy-start = (bf16[512,128]{1,0:T(8,128)(2,1)S(1)}, bf16[512,128]{1,0:T(8,128)(2,1)}, u32[]{:S(2)}) copy-start(bf16[512,128]{1,0:T(8,128)(2,1)} %get-tuple-element.8.table_ref) | copy-start | bytes 393220
  34.4 0.8 %copy-start.2 = (s32[32,256]{1,0:T(8,128)S(1)}, s32[32,256]{1,0:T(8,128)}, u32[]{:S(2)}) copy-start(s32[32,256]{1,0:T(8,128)} %get-tuple-element.9.tp_ref) | copy-start | bytes 98308
  35.2 0.8 %copy-start.3 = (s32[32,256]{1,0:T(8,128)S(1)}, s32[32,256]{1,0:T(8,128)}, u32[]{:S(2)}) copy-start(s32[32,256]{1,0:T(8,128)} %get-tuple-element.10.lp_ref) | copy-start | bytes 98308

commit v4 on v3

--- a/solution.py
+++ b/solution.py
@@ -167,89 +167,110 @@
 
 def sketch_kernel(
     tiles, me_ref, x_ref, delta_ref, pattern_ref, rs_ref, cs_ref, cols_ref, table_out, tp_out, lp_out,
-    table_ref, tp_ref, lp_ref, dt_ref, cf_ref, g_ref, t1_ref, work_ref, rank_ref, start_ref, pacc_ref, rc_ref, so_ref,
-    info_v, info_s, sem, out_sem,
+    x_buf, delta_buf, table_ref, tp_ref, lp_ref, dt_ref, cf_ref, g_ref, t1_ref, work_ref, rank_ref,
+    start_ref, pacc_ref, rc_ref, so_ref, info_v, info_s, x_sem, delta_sem, info_sem, out_sem,
 ):
-    e, nb = pl.program_id(0), pl.program_id(1)
-    examples, steps = pl.num_programs(0), pl.num_programs(1)
     bins, lanes, rows = g_ref.shape[1:]
     n_examples = t1_ref.shape[1]
     width = bins * lanes
-    tokens, step_cols = x_ref.shape[1:]
+    n_slots, tokens, step_cols = x_buf.shape
     n_steps = width // step_cols
+    all_steps = n_examples * n_steps
     per = min(rows, BLK)
     bands = rows // per
     step_blocks = step_cols // lanes
-    step = e * n_steps + nb
     n_rows = rank_ref.shape[0]
+    per_step = -(-n_rows // all_steps)
     me = me_ref[0]
 
-    @pl.when(step == 0)
-    def _():
-        count(cols_ref, rank_ref, start_ref, info_v, bins, width)
-        copy = pltpu.make_async_copy(info_v, info_s, sem)
-        copy.start()
-        pacc_ref[...] = jnp.zeros_like(pacc_ref)
-        so_ref[...] = jnp.zeros_like(so_ref)
-        for b in range(bands):
-            band = pattern_ref[pl.ds(me * rows // BLK + b, 1), :]
-            for c in range(bins):
-                factor = band[:, c : c + 1] * cs_ref[:, c * lanes : (c + 1) * lanes]
-                factor = jnp.broadcast_to(factor.astype(F32) / tokens, (per, lanes))
-                cf_ref[c, :, b * per : (b + 1) * per] = factor.T
-        copy.wait()
-
-    @pl.when(nb == 0)
-    def _():
-        span = max(rows, LANES)
-        window = rs_ref[:, pl.ds(pl.multiple_of(me * rows // span * span, span), span)]
-        own = window[:, :rows]
-        for u in range(1, span // rows):
-            own = jnp.where(me % (span // rows) == u, window[:, u * rows : (u + 1) * rows], own)
-        dt_ref[...] = delta_ref[0] * own.astype(F32).astype(BF16)
-
-    slot = lax.rem(e, 2)
-    last = lax.rem(e + n_examples - 1, n_examples)
-    butterfly(g_ref, t1_ref, work_ref, 1 - slot, last, nb, n_steps)
-
-    per_step = -(-n_rows // (n_examples * n_steps))
-    for u in range(per_step):
-        pacc_ref[...] += place(
-            step * per_step + u, cols_ref, rank_ref, start_ref, tp_ref, lp_ref, bins, width, rows, tiles
-        )
-
-    acc = lax.dot_general(x_ref[0], dt_ref[...], TN, preferred_element_type=F32)
-    for c in range(step_blocks):
-        block = acc[c * lanes : (c + 1) * lanes] * cf_ref[nb * step_blocks + c]
-        g_ref[slot, nb * step_blocks + c] = block.astype(BF16)
-
-    @pl.when(step == examples * steps - 1)
-    def _():
-        slots_out = pltpu.make_async_copy(tp_ref, tp_out, out_sem.at[0])
-        lanes_out = pltpu.make_async_copy(lp_ref, lp_out, out_sem.at[1])
-        slots_out.start()
-        lanes_out.start()
-        for q in range(n_steps):
-            butterfly(g_ref, t1_ref, work_ref, slot, e, q, n_steps)
-        for v in range(2):
-            part = pacc_ref[2 * tiles * v : 2 * tiles * (v + 1)].astype(jnp.int32)
-            rc_ref[v] = jnp.concatenate([part[:tiles], part[tiles:]], axis=1)
-
-        def four(s, carry):
-            for u in range(4):
-                tile_values(s * 4 + u, rc_ref, info_s, t1_ref, so_ref)
-            return carry
-
-        lax.fori_loop(0, (info_s[1, 0] + 3) // 4, four, 0)
-        for k in range(n_examples):
-            one = so_ref[k]
-            both = jnp.concatenate([one[:, :LANES], one[:, LANES:]], axis=0)
-            table_ref[k * LANES : (k + 1) * LANES] = both.T.astype(BF16)
-        table_copy = pltpu.make_async_copy(table_ref, table_out, out_sem.at[2])
-        table_copy.start()
-        slots_out.wait()
-        lanes_out.wait()
-        table_copy.wait()
+    def fetch(step):
+        at = pl.ds(pl.multiple_of(step % n_steps * step_cols, step_cols), step_cols)
+        slot = step % n_slots
+        return pltpu.make_async_copy(x_ref.at[step // n_steps, :, at], x_buf.at[slot], x_sem.at[slot])
+
+    def fetch_delta(e):
+        return pltpu.make_async_copy(delta_ref.at[e], delta_buf.at[e], delta_sem.at[e])
+
+    for step in range(min(n_slots, all_steps)):
+        if step % n_steps == 0:
+            fetch_delta(step // n_steps).start()
+        fetch(step).start()
+    for e in range(-(-min(n_slots, all_steps) // n_steps), n_examples):
+        fetch_delta(e).start()
+
+    count(cols_ref, rank_ref, start_ref, info_v, bins, width)
+    info_copy = pltpu.make_async_copy(info_v, info_s, info_sem)
+    info_copy.start()
+    pacc_ref[...] = jnp.zeros_like(pacc_ref)
+    so_ref[...] = jnp.zeros_like(so_ref)
+    for b in range(bands):
+        band = pattern_ref[pl.ds(me * rows // BLK + b, 1), :]
+        for c in range(bins):
+            factor = band[:, c : c + 1] * cs_ref[:, c * lanes : (c + 1) * lanes]
+            factor = jnp.broadcast_to(factor.astype(F32) / tokens, (per, lanes))
+            cf_ref[c, :, b * per : (b + 1) * per] = factor.T
+    span = max(rows, LANES)
+    window = rs_ref[:, pl.ds(pl.multiple_of(me * rows // span * span, span), span)]
+    own = window[:, :rows]
+    for u in range(1, span // rows):
+        own = jnp.where(me % (span // rows) == u, window[:, u * rows : (u + 1) * rows], own)
+    own = own.astype(F32).astype(BF16)
+
+    def one_step(step, carry):
+        e, nb = step // n_steps, step % n_steps
+        slot = e % 2
+
+        @pl.when(nb == 0)
+        def _():
+            fetch_delta(e).wait()
+            dt_ref[...] = delta_buf[e] * own
+
+        fetch(step).wait()
+        last = (e + n_examples - 1) % n_examples
+        butterfly(g_ref, t1_ref, work_ref, 1 - slot, last, nb, n_steps)
+        for u in range(per_step):
+            pacc_ref[...] += place(
+                step * per_step + u, cols_ref, rank_ref, start_ref, tp_ref, lp_ref, bins, width, rows, tiles
+            )
+        acc = lax.dot_general(x_buf[step % n_slots], dt_ref[...], TN, preferred_element_type=F32)
+        for c in range(step_blocks):
+            block = acc[c * lanes : (c + 1) * lanes] * cf_ref[nb * step_blocks + c]
+            g_ref[slot, nb * step_blocks + c] = block.astype(BF16)
+
+        @pl.when(step + n_slots < all_steps)
+        def _():
+            fetch(step + n_slots).start()
+
+        return carry
+
+    lax.fori_loop(0, all_steps, one_step, 0)
+
+    slots_out = pltpu.make_async_copy(tp_ref, tp_out, out_sem.at[0])
+    lanes_out = pltpu.make_async_copy(lp_ref, lp_out, out_sem.at[1])
+    slots_out.start()
+    lanes_out.start()
+    info_copy.wait()
+    for q in range(n_steps):
+        butterfly(g_ref, t1_ref, work_ref, (n_examples - 1) % 2, n_examples - 1, q, n_steps)
+    for v in range(2):
+        part = pacc_ref[2 * tiles * v : 2 * tiles * (v + 1)].astype(jnp.int32)
+        rc_ref[v] = jnp.concatenate([part[:tiles], part[tiles:]], axis=1)
+
+    def four(s, carry):
+        for u in range(4):
+            tile_values(s * 4 + u, rc_ref, info_s, t1_ref, so_ref)
+        return carry
+
+    lax.fori_loop(0, (info_s[1, 0] + 3) // 4, four, 0)
+    for k in range(n_examples):
+        one = so_ref[k]
+        both = jnp.concatenate([one[:, :LANES], one[:, LANES:]], axis=0)
+        table_ref[k * LANES : (k + 1) * LANES] = both.T.astype(BF16)
+    table_copy = pltpu.make_async_copy(table_ref, table_out, out_sem.at[2])
+    table_copy.start()
+    slots_out.wait()
+    lanes_out.wait()
+    table_copy.wait()
 
 
 def local_sketch(me, x_acts, delta, pattern, row_signs, col_signs, cols):
@@ -262,29 +283,24 @@
     steps = width // step_cols
     n_rows = sketch // TILE
     smem = pl.BlockSpec(memory_space=pltpu.SMEM)
-    whole = lambda shape: pl.BlockSpec(shape, lambda e, n: (0,) * len(shape))
+    hbm = pl.BlockSpec(memory_space=pltpu.HBM)
+    vmem = pl.BlockSpec(memory_space=pltpu.VMEM)
+    slots = min(8, steps * examples)
     units = LANES // steps // 16 * max(rows // LANES, 1)
     table = (examples * LANES, 2 * tiles)
     places = (n_rows, TILE)
     return pl.pallas_call(
         functools.partial(sketch_kernel, tiles),
-        grid=(examples, steps),
         out_shape=[
             jax.ShapeDtypeStruct(table, BF16),
             jax.ShapeDtypeStruct(places, jnp.int32),
             jax.ShapeDtypeStruct(places, jnp.int32),
         ],
-        in_specs=[
-            smem,
-            pl.BlockSpec((1, tokens, step_cols), lambda e, n: (e, 0, n)),
-            pl.BlockSpec((1, tokens, rows), lambda e, n: (e, 0, 0)),
-            whole(pattern.shape),
-            whole(row_signs.shape),
-            whole(col_signs.shape),
-            whole(cols.shape),
-        ],
-        out_specs=[pl.BlockSpec(memory_space=pltpu.HBM)] * 3,
+        in_specs=[smem, hbm, hbm, vmem, vmem, vmem, vmem],
+        out_specs=[hbm] * 3,
         scratch_shapes=[
+            pltpu.VMEM((slots, tokens, step_cols), BF16),
+            pltpu.VMEM((examples, tokens, rows), BF16),
             pltpu.VMEM(table, BF16),
             pltpu.VMEM(places, jnp.int32),
             pltpu.VMEM(places, jnp.int32),
@@ -300,6 +316,8 @@
             pltpu.VMEM((examples, tiles, TILE), F32),
             pltpu.VMEM((8, LANES), jnp.int32),
             pltpu.SMEM((8, LANES), jnp.int32),
+            pltpu.SemaphoreType.DMA((slots,)),
+            pltpu.SemaphoreType.DMA((examples,)),
             pltpu.SemaphoreType.DMA,
             pltpu.SemaphoreType.DMA((3,)),
         ],
@@ -313,9 +331,15 @@
 
 
 def sum_kernel(
-    n, n_examples, chunk, width, rows, table_ref, tp_ref, lp_ref, cols_ref, out_ref,
-    part, recv, send1, recv1, send2, recv2,
+    n, n_examples, chunk, width, rows, table_in, tp_in, lp_in, cols_ref, out_ref,
+    table_ref, tp_ref, lp_ref, part, recv, in_sem, send1, recv1, send2, recv2,
 ):
+    fetches = [
+        pltpu.make_async_copy(src, dst, in_sem.at[i])
+        for i, (src, dst) in enumerate([(table_in, table_ref), (tp_in, tp_ref), (lp_in, lp_ref)])
+    ]
+    for fetch in fetches:
+        fetch.start()
     me = lax.axis_index("feat")
     chunks = cols_ref.shape[1] // chunk
     pieces = n // chunks
@@ -373,6 +397,8 @@
         send(2 * o + 1)
 
     loop(1, n, greet)
+    for fetch in fetches:
+        fetch.wait()
     compute(0)
     compute(1)
     pl.semaphore_wait(barrier, n - 1)
@@ -408,11 +434,19 @@
     return pl.pallas_call(
         functools.partial(sum_kernel, n, examples, chunk, width, rows),
         out_shape=jax.ShapeDtypeStruct(shape, F32),
-        in_specs=[vmem] * 4,
+        in_specs=[pl.BlockSpec(memory_space=pltpu.HBM)] * 3 + [vmem],
         out_specs=vmem,
-        scratch_shapes=[pltpu.VMEM(shape, BF16)] * 2 + [pltpu.SemaphoreType.DMA((n,))] * 4,
+        scratch_shapes=[
+            pltpu.VMEM(table.shape, BF16),
+            pltpu.VMEM(slots.shape, jnp.int32),
+            pltpu.VMEM(slots.shape, jnp.int32),
+            pltpu.VMEM(shape, BF16),
+            pltpu.VMEM(shape, BF16),
+            pltpu.SemaphoreType.DMA((3,)),
+        ]
+        + [pltpu.SemaphoreType.DMA((n,))] * 4,
         compiler_params=pltpu.CompilerParams(
-            collective_id=0, has_side_effects=True, vmem_limit_bytes=32 * 2**20
+            collective_id=0, has_side_effects=True, vmem_limit_bytes=60 * 2**20
         ),
     )(table, slots, places, cols)
 

time: 54.3 us -> 50.4 us (0.928)
  local copies, waits for them, and re-layouts: 2.42 us -> 0 us
  Pallas kernels: 50.9 us -> 49 us
  other arithmetic: 0.67 us -> 1.57 us
    pallas_call x1, Pallas kernels: 33.5 us -> 30.1 us  [local_sketch(): pl.pallas_call(functools.partial(sketch_kernel, tiles), out_shape=[jax.Sh...]
    unnamed x8 -> x0, local copies, waits for them, and re-layouts: 2.42 us -> none
    pallas_call x1, Pallas kernels: 17.4 us -> 18.9 us  [sum_shares(): pl.pallas_call(functools.partial(sum_kernel, n, examples, chunk, width, r...]
    div x1, other arithmetic: 0.67 us -> 1.57 us  [per_device(): return total.reshape(examples, sketch) / math.sqrt(sketch)]
where the time goes in v4:
time: 50.4 us; the launch traced here: 50.6 us
  Pallas kernels  49 us (97%)
  other arithmetic  1.57 us (3%)
    pallas_call x1, Pallas kernels, local_sketch(): pl.pallas_call(functools.partial(sketch_kernel, tiles), out_shape=[jax.Sh...  30.1 us
    pallas_call x1, Pallas kernels, sum_shares(): pl.pallas_call(functools.partial(sum_kernel, n, examples, chunk, width, r...  18.9 us
    div x1, other arithmetic, per_device(): return total.reshape(examples, sketch) / math.sqrt(sketch)  1.57 us

profile of v4, /device:TPU:0, one launch (start us, length us, event | category | flops | bytes accessed | tf_op | source)
XLA Modules:
  0.0 50.6 jit_solution(7490870206582491945)
XLA Ops:
  0.0 30.1 %shard_map.64 = (bf16[512,128]{1,0:T(8,128)(2,1)}, s32[32,256]{1,0:T(8,128)}, s32[32,256]{1,0:T(8,128)}) custom-call(s32[1]{0:T(128)} %bitcast.me_ref, bf16[4,1024,4096]{2,1,0:T(8,128)(2,1)} %x_ref.1, bf16[4,1024,256]{2,1,0:T(8,128)(2,1)} %delta_ref.1, s32[32,32]{1,0:T(8,128)} %pattern_ref.1, s32[1,4096]{1,0:T(1,128)} %bitcast.11, s32[1,4096]{1,0:T(1,128)} %bitcast.12, ...), custom_call_target="tpu_custom_call" | custom-call | flops 8589934592 | bytes 35651584 | tf_op jit(solution)/shard_map/pallas_call | solution.py:292
  30.1 18.9 %shard_map.65 = f32[16,16,128]{2,1,0:T(8,128)} custom-call(bf16[512,128]{1,0:T(8,128)(2,1)} %get-tuple-element.8.table_in, s32[32,256]{1,0:T(8,128)} %get-tuple-element.9.tp_in, s32[32,256]{1,0:T(8,128)} %get-tuple-element.10.lp_in, s32[1,8192]{1,0:T(1,128)} %bitcast.10), custom_call_target="tpu_custom_call" | custom-call | tf_op jit(solution)/shard_map/pallas_call | solution.py:434
  49.0 1.6 %broadcast_multiply_fusion = f32[16,16,128]{2,1,0:T(8,128)} fusion(f32[16,16,128]{2,1,0:T(8,128)} %shard_map.65), kind=kLoop, calls=%fused_computation | loop fusion | flops 32768 | bytes 262144 | tf_op jit(solution)/shard_map/div | solution.py:467

commit v5 on v4

--- a/solution.py
+++ b/solution.py
@@ -28,8 +28,16 @@
     return value & 1
 
 
+def low(value, size):
+    return value & (size - 1)
+
+
+def high(value, size):
+    return value >> (size.bit_length() - 1)
+
+
 def sign_of(left, right, bits):
-    return (1 - 2 * parity(left & right, bits)).astype(F32)
+    return jnp.where(parity(left & right, bits) == 0, 1.0, -1.0)
 
 
 def iota(shape, axis):
@@ -37,7 +45,8 @@
 
 
 def hits(cols_ref, a, bins, width):
-    block = (cols_ref[:, pl.ds(pl.multiple_of(a * TILE, TILE), TILE)] % width) // LANES
+    cols = cols_ref[:, pl.ds(pl.multiple_of(a * TILE, TILE), TILE)]
+    block = high(low(cols, width), LANES)
     return iota((bins, TILE), 0) == block
 
 
@@ -54,7 +63,7 @@
         rank = jnp.sum(hit[a] * (here[:, :TILE] + running), axis=0, keepdims=True)
         rank_ref[a : a + 1, :] = rank.astype(jnp.int32)
         running = running + here[:, TILE:]
-    need = (running.astype(jnp.int32) + (TILE - 1)) // TILE
+    need = high(running.astype(jnp.int32) + (TILE - 1), TILE)
     lower = (iota((bins, bins), 1) < iota((bins, bins), 0)).astype(F32).astype(BF16)
     start = jnp.dot(lower, need.astype(F32).astype(BF16), preferred_element_type=F32)
     start_ref[...] = start
@@ -72,14 +81,14 @@
         jnp.where(hits(cols_ref, a, bins, width), start_ref[...], 0.0), axis=0, keepdims=True
     )
     rank = rank_ref[pl.ds(a, 1), :]
-    lane = rank % TILE
-    slot = first.astype(jnp.int32) + rank // TILE + (lane // LANES) * tiles
-    lane = lane % LANES
+    lane = low(rank, TILE)
+    slot = first.astype(jnp.int32) + high(rank, TILE) + high(lane, LANES) * tiles
+    lane = low(lane, LANES)
     tp_ref[pl.ds(a, 1), :] = slot
     lp_ref[pl.ds(a, 1), :] = lane
     cols = cols_ref[:, pl.ds(pl.multiple_of(a * TILE, TILE), TILE)]
-    row = ((cols // width) % rows).astype(F32)
-    col = (cols % LANES).astype(F32)
+    row = low(high(cols, width), rows).astype(F32)
+    col = low(cols, LANES).astype(F32)
     here = iota((slots, TILE), 0) == slot
     left = jnp.concatenate([jnp.where(here, row, 0.0), jnp.where(here, col, 0.0)], axis=0)
     right = (iota((LANES, TILE), 0) == lane).astype(F32)
@@ -125,14 +134,14 @@
     row = rc_ref[0, pl.ds(t, 1), :]
     col = rc_ref[1, pl.ds(t, 1), :]
     low_ids = iota((16, TILE), 0)
-    row_low = sign_of(low_ids, row % 16, 4).astype(BF16)
-    high_bits = rows // 16
-    row_high = sign_of(iota((max(high_bits, 8), TILE), 0), row // 16, 8).astype(BF16)
-    weight = jnp.concatenate([row_low * row_high[h : h + 1] for h in range(high_bits)], axis=0)
+    row_low = sign_of(low_ids, low(row, 16), 4).astype(BF16)
+    outer = rows // 16
+    row_high = sign_of(iota((max(outer, 8), TILE), 0), high(row, 16), outer.bit_length()).astype(BF16)
+    weight = jnp.concatenate([row_low * row_high[h : h + 1] for h in range(outer)], axis=0)
     block = t1_ref[info_s[0, t]].reshape(examples * LANES, rows)
     value = jnp.dot(block, weight, preferred_element_type=F32)
-    col_low = sign_of(iota((8, TILE), 0), col % 8, 3)
-    col_high = sign_of(iota((16, TILE), 0), col // 8, 4)
+    col_low = sign_of(iota((8, TILE), 0), low(col, 8), 3)
+    col_high = sign_of(iota((16, TILE), 0), high(col, 8), 4)
     for e in range(examples):
         total = jnp.zeros((8, TILE), F32)
         for h in range(16):
@@ -147,22 +156,20 @@
     def wide(ref):
         return jnp.concatenate([ref[pl.ds(per * a + u, 1), :] for u in range(per)], axis=1)
 
-    pick = (iota((table_ref.shape[1], chunk), 0) == wide(tp_ref)).astype(F32).astype(BF16)
+    slots = table_ref.shape[1] // 2
+    pick = (iota((slots, chunk), 0) == wide(tp_ref)).astype(F32).astype(BF16)
+    pick = jnp.concatenate([pick, pick], axis=0)
     spread = jnp.dot(table_ref[...], pick, preferred_element_type=F32)
     mine = iota((LANES, chunk), 0) == wide(lp_ref)
-    high = cols_ref[:, pl.ds(pl.multiple_of(a * chunk, chunk), chunk)] // (width * rows)
-    sign = sign_of(high, me, 16)
+    cols = cols_ref[:, pl.ds(pl.multiple_of(a * chunk, chunk), chunk)]
+    sign = sign_of(high(cols, width * rows), me, 16)
     kept = [
         jnp.sum(jnp.where(mine, spread[e * LANES : (e + 1) * LANES], 0.0), axis=0, keepdims=True)
-        * sign
         for e in range(n_examples)
     ]
-    lines = [
-        kept[e][:, q * LANES : (q + 1) * LANES]
-        for q in range(chunk // LANES)
-        for e in range(n_examples)
-    ]
-    return jnp.concatenate(lines, axis=0).astype(BF16)
+    kept = jnp.concatenate(kept, axis=0) * sign
+    lines = [kept[:, q * LANES : (q + 1) * LANES] for q in range(chunk // LANES)]
+    return jnp.concatenate(lines, axis=0)
 
 
 def sketch_kernel(
@@ -184,9 +191,9 @@
     me = me_ref[0]
 
     def fetch(step):
-        at = pl.ds(pl.multiple_of(step % n_steps * step_cols, step_cols), step_cols)
-        slot = step % n_slots
-        return pltpu.make_async_copy(x_ref.at[step // n_steps, :, at], x_buf.at[slot], x_sem.at[slot])
+        at = pl.ds(pl.multiple_of(low(step, n_steps) * step_cols, step_cols), step_cols)
+        slot = low(step, n_slots)
+        return pltpu.make_async_copy(x_ref.at[high(step, n_steps), :, at], x_buf.at[slot], x_sem.at[slot])
 
     def fetch_delta(e):
         return pltpu.make_async_copy(delta_ref.at[e], delta_buf.at[e], delta_sem.at[e])
@@ -204,21 +211,21 @@
     pacc_ref[...] = jnp.zeros_like(pacc_ref)
     so_ref[...] = jnp.zeros_like(so_ref)
     for b in range(bands):
-        band = pattern_ref[pl.ds(me * rows // BLK + b, 1), :]
+        band = pattern_ref[pl.ds(high(me * rows, BLK) + b, 1), :]
         for c in range(bins):
             factor = band[:, c : c + 1] * cs_ref[:, c * lanes : (c + 1) * lanes]
             factor = jnp.broadcast_to(factor.astype(F32) / tokens, (per, lanes))
             cf_ref[c, :, b * per : (b + 1) * per] = factor.T
     span = max(rows, LANES)
-    window = rs_ref[:, pl.ds(pl.multiple_of(me * rows // span * span, span), span)]
+    window = rs_ref[:, pl.ds(pl.multiple_of(high(me * rows, span) * span, span), span)]
     own = window[:, :rows]
     for u in range(1, span // rows):
-        own = jnp.where(me % (span // rows) == u, window[:, u * rows : (u + 1) * rows], own)
+        own = jnp.where(low(me, span // rows) == u, window[:, u * rows : (u + 1) * rows], own)
     own = own.astype(F32).astype(BF16)
 
     def one_step(step, carry):
-        e, nb = step // n_steps, step % n_steps
-        slot = e % 2
+        e, nb = high(step, n_steps), low(step, n_steps)
+        slot = low(e, 2)
 
         @pl.when(nb == 0)
         def _():
@@ -226,13 +233,13 @@
             dt_ref[...] = delta_buf[e] * own
 
         fetch(step).wait()
-        last = (e + n_examples - 1) % n_examples
+        last = low(e + n_examples - 1, n_examples)
         butterfly(g_ref, t1_ref, work_ref, 1 - slot, last, nb, n_steps)
         for u in range(per_step):
             pacc_ref[...] += place(
                 step * per_step + u, cols_ref, rank_ref, start_ref, tp_ref, lp_ref, bins, width, rows, tiles
             )
-        acc = lax.dot_general(x_buf[step % n_slots], dt_ref[...], TN, preferred_element_type=F32)
+        acc = lax.dot_general(x_buf[low(step, n_slots)], dt_ref[...], TN, preferred_element_type=F32)
         for c in range(step_blocks):
             block = acc[c * lanes : (c + 1) * lanes] * cf_ref[nb * step_blocks + c]
             g_ref[slot, nb * step_blocks + c] = block.astype(BF16)
@@ -261,11 +268,14 @@
             tile_values(s * 4 + u, rc_ref, info_s, t1_ref, so_ref)
         return carry
 
-    lax.fori_loop(0, (info_s[1, 0] + 3) // 4, four, 0)
+    lax.fori_loop(0, high(info_s[1, 0] + 3, 4), four, 0)
     for k in range(n_examples):
         one = so_ref[k]
         both = jnp.concatenate([one[:, :LANES], one[:, LANES:]], axis=0)
-        table_ref[k * LANES : (k + 1) * LANES] = both.T.astype(BF16)
+        both = both.T
+        coarse = both.astype(BF16)
+        fine = (both - coarse.astype(F32)).astype(BF16)
+        table_ref[k * LANES : (k + 1) * LANES] = jnp.concatenate([coarse, fine], axis=1)
     table_copy = pltpu.make_async_copy(table_ref, table_out, out_sem.at[2])
     table_copy.start()
     slots_out.wait()
@@ -287,7 +297,7 @@
     vmem = pl.BlockSpec(memory_space=pltpu.VMEM)
     slots = min(8, steps * examples)
     units = LANES // steps // 16 * max(rows // LANES, 1)
-    table = (examples * LANES, 2 * tiles)
+    table = (examples * LANES, 4 * tiles)
     places = (n_rows, TILE)
     return pl.pallas_call(
         functools.partial(sketch_kernel, tiles),
@@ -409,9 +419,9 @@
     def collect(o, total):
         source = other(n - o)
         share(part.at[source], recv.at[source], send1.at[source], recv1.at[source], source).wait_recv()
-        return total + recv[source].astype(F32)
-
-    out_ref[me] = lax.fori_loop(1, n, collect, part[me].astype(F32))
+        return total + recv[source]
+
+    out_ref[me] = lax.fori_loop(1, n, collect, part[me]).astype(BF16)
 
     def spread(o):
         to = other(o)
@@ -433,20 +443,20 @@
     shape = (n, cols.shape[1] // n * examples // LANES, LANES)
     return pl.pallas_call(
         functools.partial(sum_kernel, n, examples, chunk, width, rows),
-        out_shape=jax.ShapeDtypeStruct(shape, F32),
+        out_shape=jax.ShapeDtypeStruct(shape, BF16),
         in_specs=[pl.BlockSpec(memory_space=pltpu.HBM)] * 3 + [vmem],
         out_specs=vmem,
         scratch_shapes=[
             pltpu.VMEM(table.shape, BF16),
             pltpu.VMEM(slots.shape, jnp.int32),
             pltpu.VMEM(slots.shape, jnp.int32),
-            pltpu.VMEM(shape, BF16),
-            pltpu.VMEM(shape, BF16),
+            pltpu.VMEM(shape, F32),
+            pltpu.VMEM(shape, F32),
             pltpu.SemaphoreType.DMA((3,)),
         ]
         + [pltpu.SemaphoreType.DMA((n,))] * 4,
         compiler_params=pltpu.CompilerParams(
-            collective_id=0, has_side_effects=True, vmem_limit_bytes=60 * 2**20
+            collective_id=0, has_side_effects=True, vmem_limit_bytes=32 * 2**20
         ),
     )(table, slots, places, cols)
 
@@ -464,7 +474,7 @@
     )
     total = sum_shares(table, slots, places, cols, n, examples, chunk, width, rows)
     total = total.reshape(sketch // chunk, chunk // LANES, examples, LANES).transpose(2, 0, 1, 3)
-    return total.reshape(examples, sketch) / math.sqrt(sketch)
+    return total.reshape(examples, sketch).astype(F32) / math.sqrt(sketch)
 
 
 def solution(mesh):

time: 50.4 us -> 50.9 us (level); the launches traced: 50.6 us -> 50.5 us
  local copies, waits for them, and re-layouts: 0 us -> 2.46 us
  Pallas kernels: 49 us -> 47.4 us
  other arithmetic: 1.57 us -> 0.67 us
    unnamed x0 -> x8, local copies, waits for them, and re-layouts: none -> 2.46 us
    pallas_call x1, Pallas kernels: 18.9 us -> 17.8 us  [sum_shares(): pl.pallas_call(functools.partial(sum_kernel, n, examples, chunk, width, r...]
    div x1, other arithmetic: 1.57 us -> 0.67 us  [per_device(): return total.reshape(examples, sketch).astype(F32) / math.sqrt(sketch)]
    pallas_call x1, Pallas kernels: 30.1 us -> 29.6 us  [local_sketch(): pl.pallas_call(functools.partial(sketch_kernel, tiles), out_shape=[jax.Sh...]
where the time goes in v5:
time: 50.9 us; the launch traced here: 50.5 us
  Pallas kernels  47.4 us (93%)
  local copies, waits for them, and re-layouts  2.46 us (5%)
  other arithmetic  0.67 us (1%)
    pallas_call x1, Pallas kernels, local_sketch(): pl.pallas_call(functools.partial(sketch_kernel, tiles), out_shape=[jax.Sh...  29.6 us
    pallas_call x1, Pallas kernels, sum_shares(): pl.pallas_call(functools.partial(sum_kernel, n, examples, chunk, width, r...  17.8 us
    unnamed x8, local copies, waits for them, and re-layouts  2.46 us

profile of v5, /device:TPU:0, one launch (start us, length us, event | category | flops | bytes accessed | tf_op | source)
XLA Modules:
  0.0 50.5 jit_solution(8211179908369421718)
XLA Ops:
  0.0 0.0 copy-start.1
  0.0 29.6 %shard_map.64 = (bf16[512,256]{1,0:T(8,128)(2,1)}, s32[32,256]{1,0:T(8,128)}, s32[32,256]{1,0:T(8,128)}) custom-call(s32[1]{0:T(128)} %bitcast.me_ref, bf16[4,1024,4096]{2,1,0:T(8,128)(2,1)} %x_ref.1, bf16[4,1024,256]{2,1,0:T(8,128)(2,1)} %delta_ref.1, s32[32,32]{1,0:T(8,128)} %pattern_ref.1, s32[1,4096]{1,0:T(1,128)} %bitcast.11, s32[1,4096]{1,0:T(1,128)} %bitcast.12, ...), custom_call_target="tpu_custom_call" | custom-call | flops 8589934592 | bytes 35651584 | tf_op jit(solution)/shard_map/pallas_call | solution.py:302
  29.6 0.0 copy-done.1
  29.6 0.0 copy-start
  29.6 0.9 %copy-done = bf16[512,256]{1,0:T(8,128)(2,1)S(1)} copy-done((bf16[512,256]{1,0:T(8,128)(2,1)S(1)}, bf16[512,256]{1,0:T(8,128)(2,1)}, u32[]{:S(2)}) %copy-start) | copy-done | bytes 262168
  30.6 0.0 copy-start.2
  30.6 0.8 %copy-done.2 = s32[32,256]{1,0:T(8,128)S(1)} copy-done((s32[32,256]{1,0:T(8,128)S(1)}, s32[32,256]{1,0:T(8,128)}, u32[]{:S(2)}) %copy-start.2) | copy-done | bytes 32792
  31.3 0.0 copy-start.3
  31.3 0.8 %copy-done.3 = s32[32,256]{1,0:T(8,128)S(1)} copy-done((s32[32,256]{1,0:T(8,128)S(1)}, s32[32,256]{1,0:T(8,128)}, u32[]{:S(2)}) %copy-start.3) | copy-done | bytes 32792
  32.1 17.8 %shard_map.65 = bf16[16,16,128]{2,1,0:T(8,128)(2,1)S(1)} custom-call(bf16[512,256]{1,0:T(8,128)(2,1)S(1)} %copy-done, s32[32,256]{1,0:T(8,128)S(1)} %copy-done.2, s32[32,256]{1,0:T(8,128)S(1)} %copy-done.3, s32[1,8192]{1,0:T(1,128)S(1)} %bitcast.10), custom_call_target="tpu_custom_call" | custom-call | tf_op jit(solution)/shard_map/pallas_call | solution.py:444
  49.9 0.7 %convert_multiply_fusion = f32[16,16,128]{2,1,0:T(8,128)} fusion(bf16[16,16,128]{2,1,0:T(8,128)(2,1)S(1)} %shard_map.65), kind=kLoop, calls=%fused_computation | loop fusion | flops 65536 | bytes 196608 | tf_op jit(solution)/shard_map/div | solution.py:477
Async XLA Ops:
  0.0 29.6 %copy-start.1 = (s32[8192]{0:T(1024)S(1)}, s32[8192]{0:T(1024)}, u32[]{:S(2)}) copy-start(s32[8192]{0:T(1024)} %param.11) | copy-start | bytes 98308
  29.6 1.0 %copy-start = (bf16[512,256]{1,0:T(8,128)(2,1)S(1)}, bf16[512,256]{1,0:T(8,128)(2,1)}, u32[]{:S(2)}) copy-start(bf16[512,256]{1,0:T(8,128)(2,1)} %get-tuple-element.8.table_in) | copy-start | bytes 786436
  30.6 0.8 %copy-start.2 = (s32[32,256]{1,0:T(8,128)S(1)}, s32[32,256]{1,0:T(8,128)}, u32[]{:S(2)}) copy-start(s32[32,256]{1,0:T(8,128)} %get-tuple-element.9.tp_in) | copy-start | bytes 98308
  31.3 0.8 %copy-start.3 = (s32[32,256]{1,0:T(8,128)S(1)}, s32[32,256]{1,0:T(8,128)}, u32[]{:S(2)}) copy-start(s32[32,256]{1,0:T(8,128)} %get-tuple-element.10.lp_in) | copy-start | bytes 98308

commit v6 on v5

--- a/solution.py
+++ b/solution.py
@@ -12,6 +12,7 @@
 LANES = 128
 TILE = 256
 CHUNK = 512
+HALVES = 2
 F32 = jnp.float32
 BF16 = jnp.bfloat16
 NT = (((1,), (1,)), ((), ()))
@@ -108,11 +109,10 @@
     return parts
 
 
-def butterfly(g_ref, t1_ref, work_ref, slot, e, step, steps):
+def butterfly(g_ref, t1_ref, work_ref, slot, e, step, steps, unit=0):
     bins, lanes, rows = g_ref.shape[1:]
     share = lanes // steps
     wide = min(rows, LANES)
-    unit = 0
     for j in range(share // 16):
         at = pl.ds(pl.multiple_of(step * share + j * 16, 16), 16)
         for h in range(rows // wide):
@@ -129,20 +129,22 @@
             unit += 1
 
 
-def tile_values(t, rc_ref, info_s, t1_ref, so_ref):
+def tile_product(t, rc_ref, info_s, t1_ref):
     examples, _, rows = t1_ref.shape[1:]
     row = rc_ref[0, pl.ds(t, 1), :]
-    col = rc_ref[1, pl.ds(t, 1), :]
-    low_ids = iota((16, TILE), 0)
-    row_low = sign_of(low_ids, low(row, 16), 4).astype(BF16)
+    row_low = sign_of(iota((16, TILE), 0), low(row, 16), 4).astype(BF16)
     outer = rows // 16
     row_high = sign_of(iota((max(outer, 8), TILE), 0), high(row, 16), outer.bit_length()).astype(BF16)
     weight = jnp.concatenate([row_low * row_high[h : h + 1] for h in range(outer)], axis=0)
     block = t1_ref[info_s[0, t]].reshape(examples * LANES, rows)
-    value = jnp.dot(block, weight, preferred_element_type=F32)
+    return jnp.dot(block, weight, preferred_element_type=F32)
+
+
+def tile_sums(t, value, rc_ref, so_ref):
+    col = rc_ref[1, pl.ds(t, 1), :]
     col_low = sign_of(iota((8, TILE), 0), low(col, 8), 3)
     col_high = sign_of(iota((16, TILE), 0), high(col, 8), 4)
-    for e in range(examples):
+    for e in range(so_ref.shape[0]):
         total = jnp.zeros((8, TILE), F32)
         for h in range(16):
             at = e * LANES + h * 8
@@ -150,17 +152,20 @@
         so_ref[e, pl.ds(t, 1), :] = jnp.sum(total * col_low, axis=0, keepdims=True)
 
 
-def entries(a, me, table_ref, tp_ref, lp_ref, cols_ref, n_examples, chunk, width, rows):
+def wide_row(ref, a, chunk):
     per = chunk // TILE
-
-    def wide(ref):
-        return jnp.concatenate([ref[pl.ds(per * a + u, 1), :] for u in range(per)], axis=1)
-
+    return jnp.concatenate([ref[pl.ds(per * a + u, 1), :] for u in range(per)], axis=1)
+
+
+def entries(a, table_ref, tp_ref, chunk):
     slots = table_ref.shape[1] // 2
-    pick = (iota((slots, chunk), 0) == wide(tp_ref)).astype(F32).astype(BF16)
+    pick = (iota((slots, chunk), 0) == wide_row(tp_ref, a, chunk)).astype(F32).astype(BF16)
     pick = jnp.concatenate([pick, pick], axis=0)
-    spread = jnp.dot(table_ref[...], pick, preferred_element_type=F32)
-    mine = iota((LANES, chunk), 0) == wide(lp_ref)
+    return jnp.dot(table_ref[...], pick, preferred_element_type=F32)
+
+
+def chosen(a, me, spread, lp_ref, cols_ref, n_examples, chunk, width, rows):
+    mine = iota((LANES, chunk), 0) == wide_row(lp_ref, a, chunk)
     cols = cols_ref[:, pl.ds(pl.multiple_of(a * chunk, chunk), chunk)]
     sign = sign_of(high(cols, width * rows), me, 16)
     kept = [
@@ -234,15 +239,24 @@
 
         fetch(step).wait()
         last = low(e + n_examples - 1, n_examples)
-        butterfly(g_ref, t1_ref, work_ref, 1 - slot, last, nb, n_steps)
-        for u in range(per_step):
-            pacc_ref[...] += place(
-                step * per_step + u, cols_ref, rank_ref, start_ref, tp_ref, lp_ref, bins, width, rows, tiles
+        x_slot = low(step, n_slots)
+        cut = step_cols // HALVES
+        for half in range(HALVES):
+            acc = lax.dot_general(
+                x_buf[x_slot, :, half * cut : (half + 1) * cut], dt_ref[...], TN, preferred_element_type=F32
             )
-        acc = lax.dot_general(x_buf[low(step, n_slots)], dt_ref[...], TN, preferred_element_type=F32)
-        for c in range(step_blocks):
-            block = acc[c * lanes : (c + 1) * lanes] * cf_ref[nb * step_blocks + c]
-            g_ref[slot, nb * step_blocks + c] = block.astype(BF16)
+            butterfly(
+                g_ref, t1_ref, work_ref, 1 - slot, last, nb * HALVES + half, n_steps * HALVES,
+                half * work_ref.shape[0] // HALVES,
+            )
+            for u in range(half, per_step, HALVES):
+                pacc_ref[...] += place(
+                    step * per_step + u, cols_ref, rank_ref, start_ref, tp_ref, lp_ref, bins, width, rows, tiles
+                )
+            first = nb * step_blocks + half * step_blocks // HALVES
+            for c in range(step_blocks // HALVES):
+                block = acc[c * lanes : (c + 1) * lanes] * cf_ref[first + c]
+                g_ref[slot, first + c] = block.astype(BF16)
 
         @pl.when(step + n_slots < all_steps)
         def _():
@@ -263,12 +277,16 @@
         part = pacc_ref[2 * tiles * v : 2 * tiles * (v + 1)].astype(jnp.int32)
         rc_ref[v] = jnp.concatenate([part[:tiles], part[tiles:]], axis=1)
 
-    def four(s, carry):
-        for u in range(4):
-            tile_values(s * 4 + u, rc_ref, info_s, t1_ref, so_ref)
+    def eight(s, carry):
+        value = tile_product(s * 8, rc_ref, info_s, t1_ref)
+        for u in range(8):
+            now = value
+            if u < 7:
+                value = tile_product(s * 8 + u + 1, rc_ref, info_s, t1_ref)
+            tile_sums(s * 8 + u, now, rc_ref, so_ref)
         return carry
 
-    lax.fori_loop(0, high(info_s[1, 0] + 3, 4), four, 0)
+    lax.fori_loop(0, high(info_s[1, 0] + 7, 8), eight, 0)
     for k in range(n_examples):
         one = so_ref[k]
         both = jnp.concatenate([one[:, :LANES], one[:, LANES:]], axis=0)
@@ -357,7 +375,7 @@
     barrier = pltpu.get_barrier_semaphore()
 
     def other(o):
-        return lax.rem(me + o, n)
+        return me ^ (n - o)
 
     def loop(first, last, step):
         def body(o, carry):
@@ -382,15 +400,15 @@
         )
 
     def chunk_at(o):
-        return lax.rem(me // pieces + 1 + o, chunks)
-
-    def compute(o):
-        a = chunk_at(o)
-        found = entries(
-            a, me, table_ref, tp_ref, lp_ref, cols_ref, n_examples, chunk, width, rows
-        )
-        for p in range(pieces):
-            part[a * pieces + p] = found[p * lines : (p + 1) * lines]
+        return high(me, pieces) ^ (chunks - 1 - o)
+
+    def compute(first):
+        spread = [entries(chunk_at(first + u), table_ref, tp_ref, chunk) for u in range(2)]
+        for u in range(2):
+            a = chunk_at(first + u)
+            found = chosen(a, me, spread[u], lp_ref, cols_ref, n_examples, chunk, width, rows)
+            for p in range(pieces):
+                part[a * pieces + p] = found[p * lines : (p + 1) * lines]
 
     def send(o):
         for p in range(pieces):
@@ -402,7 +420,6 @@
 
     def step(o):
         compute(2 * o)
-        compute(2 * o + 1)
         send(2 * o)
         send(2 * o + 1)
 
@@ -410,14 +427,13 @@
     for fetch in fetches:
         fetch.wait()
     compute(0)
-    compute(1)
     pl.semaphore_wait(barrier, n - 1)
     send(0)
     send(1)
     loop(1, chunks // 2, step)
 
     def collect(o, total):
-        source = other(n - o)
+        source = other(o)
         share(part.at[source], recv.at[source], send1.at[source], recv1.at[source], source).wait_recv()
         return total + recv[source]
 
@@ -430,7 +446,7 @@
     loop(1, n, spread)
 
     def finish(o):
-        to, source = other(o), other(n - o)
+        to, source = other(o), other(o)
         share(part.at[to], recv.at[me], send1.at[to], recv1.at[me], to).wait_send()
         share(out_ref.at[me], out_ref.at[me], send2.at[to], recv2.at[me], to).wait_send()
         share(out_ref.at[source], out_ref.at[source], send2.at[source], recv2.at[source], source).wait_recv()
@@ -456,7 +472,7 @@
         ]
         + [pltpu.SemaphoreType.DMA((n,))] * 4,
         compiler_params=pltpu.CompilerParams(
-            collective_id=0, has_side_effects=True, vmem_limit_bytes=32 * 2**20
+            collective_id=0, has_side_effects=True, vmem_limit_bytes=60 * 2**20
         ),
     )(table, slots, places, cols)
 

time: 50.9 us -> 49 us (0.963)
  local copies, waits for them, and re-layouts: 2.46 us -> 0 us
  other arithmetic: 0.67 us -> 1.51 us
    unnamed x8 -> x0, local copies, waits for them, and re-layouts: 2.46 us -> none
    div x1, other arithmetic: 0.67 us -> 1.51 us  [per_device(): return total.reshape(examples, sketch).astype(F32) / math.sqrt(sketch)]
where the time goes in v6:
time: 49 us; the launch traced here: 48.7 us
  Pallas kernels  47.2 us (96%)
  other arithmetic  1.51 us (3%)
    pallas_call x1, Pallas kernels, local_sketch(): pl.pallas_call(functools.partial(sketch_kernel, tiles), out_shape=[jax.Sh...  29.8 us
    pallas_call x1, Pallas kernels, sum_shares(): pl.pallas_call(functools.partial(sum_kernel, n, examples, chunk, width, r...  17.4 us
    div x1, other arithmetic, per_device(): return total.reshape(examples, sketch).astype(F32) / math.sqrt(sketch)  1.51 us

profile of v6, /device:TPU:0, one launch (start us, length us, event | category | flops | bytes accessed | tf_op | source)
XLA Modules:
  0.0 48.7 jit_solution(4229296101848731221)
XLA Ops:
  0.0 29.8 %shard_map.64 = (bf16[512,256]{1,0:T(8,128)(2,1)}, s32[32,256]{1,0:T(8,128)}, s32[32,256]{1,0:T(8,128)}) custom-call(s32[1]{0:T(128)} %bitcast.me_ref, bf16[4,1024,4096]{2,1,0:T(8,128)(2,1)} %x_ref.1, bf16[4,1024,256]{2,1,0:T(8,128)(2,1)} %delta_ref.1, s32[32,32]{1,0:T(8,128)} %pattern_ref.1, s32[1,4096]{1,0:T(1,128)} %bitcast.11, s32[1,4096]{1,0:T(1,128)} %bitcast.12, ...), custom_call_target="tpu_custom_call" | custom-call | flops 8589934592 | bytes 35651584 | tf_op jit(solution)/shard_map/pallas_call | solution.py:320
  29.8 17.4 %shard_map.65 = bf16[16,16,128]{2,1,0:T(8,128)(2,1)} custom-call(bf16[512,256]{1,0:T(8,128)(2,1)} %get-tuple-element.8.table_in, s32[32,256]{1,0:T(8,128)} %get-tuple-element.9.tp_in, s32[32,256]{1,0:T(8,128)} %get-tuple-element.10.lp_in, s32[1,8192]{1,0:T(1,128)} %bitcast.10), custom_call_target="tpu_custom_call" | custom-call | tf_op jit(solution)/shard_map/pallas_call | solution.py:460
  47.2 1.5 %convert_multiply_fusion = f32[16,16,128]{2,1,0:T(8,128)} fusion(bf16[16,16,128]{2,1,0:T(8,128)(2,1)} %shard_map.65), kind=kLoop, calls=%fused_computation | loop fusion | flops 65536 | bytes 196608 | tf_op jit(solution)/shard_map/div | solution.py:493

commit v7 on v6

--- a/solution.py
+++ b/solution.py
@@ -16,7 +16,6 @@
 F32 = jnp.float32
 BF16 = jnp.bfloat16
 NT = (((1,), (1,)), ((), ()))
-TN = (((0,), (0,)), ((), ()))
 
 
 def parity(value, bits):
@@ -219,8 +218,8 @@
         band = pattern_ref[pl.ds(high(me * rows, BLK) + b, 1), :]
         for c in range(bins):
             factor = band[:, c : c + 1] * cs_ref[:, c * lanes : (c + 1) * lanes]
-            factor = jnp.broadcast_to(factor.astype(F32) / tokens, (per, lanes))
-            cf_ref[c, :, b * per : (b + 1) * per] = factor.T
+            at = c * lanes % step_cols
+            cf_ref[c * lanes // step_cols, b : b + 1, at : at + lanes] = factor.astype(F32) / tokens
     span = max(rows, LANES)
     window = rs_ref[:, pl.ds(pl.multiple_of(high(me * rows, span) * span, span), span)]
     own = window[:, :rows]
@@ -235,15 +234,15 @@
         @pl.when(nb == 0)
         def _():
             fetch_delta(e).wait()
-            dt_ref[...] = delta_buf[e] * own
+            dt_ref[...] = (delta_buf[e] * own).T
 
         fetch(step).wait()
         last = low(e + n_examples - 1, n_examples)
         x_slot = low(step, n_slots)
         cut = step_cols // HALVES
         for half in range(HALVES):
-            acc = lax.dot_general(
-                x_buf[x_slot, :, half * cut : (half + 1) * cut], dt_ref[...], TN, preferred_element_type=F32
+            acc = jnp.dot(
+                dt_ref[...], x_buf[x_slot, :, half * cut : (half + 1) * cut], preferred_element_type=F32
             )
             butterfly(
                 g_ref, t1_ref, work_ref, 1 - slot, last, nb * HALVES + half, n_steps * HALVES,
@@ -254,9 +253,14 @@
                     step * per_step + u, cols_ref, rank_ref, start_ref, tp_ref, lp_ref, bins, width, rows, tiles
                 )
             first = nb * step_blocks + half * step_blocks // HALVES
+            factor = cf_ref[nb, :, half * cut : (half + 1) * cut]
             for c in range(step_blocks // HALVES):
-                block = acc[c * lanes : (c + 1) * lanes] * cf_ref[first + c]
-                g_ref[slot, first + c] = block.astype(BF16)
+                at = slice(c * lanes, (c + 1) * lanes)
+                block = [
+                    (acc[b * per : (b + 1) * per, at] * factor[b : b + 1, at]).astype(BF16)
+                    for b in range(bands)
+                ]
+                g_ref[slot, first + c] = jnp.concatenate(block, axis=0).T
 
         @pl.when(step + n_slots < all_steps)
         def _():
@@ -332,8 +336,8 @@
             pltpu.VMEM(table, BF16),
             pltpu.VMEM(places, jnp.int32),
             pltpu.VMEM(places, jnp.int32),
-            pltpu.VMEM((tokens, rows), BF16),
-            pltpu.VMEM((bins, LANES, rows), F32),
+            pltpu.VMEM((rows, tokens), BF16),
+            pltpu.VMEM((steps, max(rows // BLK, 1), step_cols), F32),
             pltpu.VMEM((2, bins, LANES, rows), BF16),
             pltpu.VMEM((bins, examples, LANES, rows), BF16),
             pltpu.VMEM((units, bins, 16, min(rows, LANES)), F32),

time: 49 us -> 47.4 us (0.967)
  Pallas kernels: 47.2 us -> 45.5 us
    pallas_call x1, Pallas kernels: 29.8 us -> 28.1 us  [local_sketch(): pl.pallas_call(functools.partial(sketch_kernel, tiles), out_shape=[jax.Sh...]
where the time goes in v7:
time: 47.4 us; the launch traced here: 47.1 us
  Pallas kernels  45.5 us (96%)
  other arithmetic  1.51 us (3%)
    pallas_call x1, Pallas kernels, local_sketch(): pl.pallas_call(functools.partial(sketch_kernel, tiles), out_shape=[jax.Sh...  28.1 us
    pallas_call x1, Pallas kernels, sum_shares(): pl.pallas_call(functools.partial(sum_kernel, n, examples, chunk, width, r...  17.4 us
    div x1, other arithmetic, per_device(): return total.reshape(examples, sketch).astype(F32) / math.sqrt(sketch)  1.51 us

profile of v7, /device:TPU:0, one launch (start us, length us, event | category | flops | bytes accessed | tf_op | source)
XLA Modules:
  0.0 47.1 jit_solution(17606277997267078900)
XLA Ops:
  0.0 28.1 %shard_map.64 = (bf16[512,256]{1,0:T(8,128)(2,1)}, s32[32,256]{1,0:T(8,128)}, s32[32,256]{1,0:T(8,128)}) custom-call(s32[1]{0:T(128)} %bitcast.me_ref, bf16[4,1024,4096]{2,1,0:T(8,128)(2,1)} %x_ref.1, bf16[4,1024,256]{2,1,0:T(8,128)(2,1)} %delta_ref.1, s32[32,32]{1,0:T(8,128)} %pattern_ref.1, s32[1,4096]{1,0:T(1,128)} %bitcast.11, s32[1,4096]{1,0:T(1,128)} %bitcast.12, ...), custom_call_target="tpu_custom_call" | custom-call | flops 8589934592 | bytes 35651584 | tf_op jit(solution)/shard_map/pallas_call | solution.py:324
  28.1 17.4 %shard_map.65 = bf16[16,16,128]{2,1,0:T(8,128)(2,1)} custom-call(bf16[512,256]{1,0:T(8,128)(2,1)} %get-tuple-element.8.table_in, s32[32,256]{1,0:T(8,128)} %get-tuple-element.9.tp_in, s32[32,256]{1,0:T(8,128)} %get-tuple-element.10.lp_in, s32[1,8192]{1,0:T(1,128)} %bitcast.10), custom_call_target="tpu_custom_call" | custom-call | tf_op jit(solution)/shard_map/pallas_call | solution.py:464
  45.5 1.5 %convert_multiply_fusion = f32[16,16,128]{2,1,0:T(8,128)} fusion(bf16[16,16,128]{2,1,0:T(8,128)(2,1)} %shard_map.65), kind=kLoop, calls=%fused_computation | loop fusion | flops 65536 | bytes 196608 | tf_op jit(solution)/shard_map/div | solution.py:497
